TPU v7x, 256 devices: a whole 4x4x8 slice. The times are simulated.
256 devices in a mesh: mp: 16 (over x, z_hi, core), scen: 16 (over z_lo, y).
Axes of the slice: x: 4, y: 4, z: 8 (z_hi: 2, z_lo: 4; z = z_hi * 4 + z_lo), core: 2. Of those that a mesh axis runs over, the one named last changes fastest.
Arguments:
- group_id: int32 [16384], P('mp'), may hold values from 0 to 255
- issue_state: int32 [16384], P('mp'), may hold values from 0 to 7
- account_start: float32 [16384], P('mp'), may hold values from 0.3 to 3
- transition: float32 [256, 8, 8], replicated, may hold values from 0 to 1
- lapse_base: float32 [256], replicated, may hold values from 0.005 to 0.05
- benefit: float32 [8], replicated, may hold values from 0.002 to 0.05
- bond_block: int32 [40960, 1], P('mp'), may hold values from 0 to 255
- bond_flows: float32 [40960, 256], P('mp'), may hold values from 0 to 0.02
- bond_target: float32 [40960], P('mp'), may hold values from 0.7 to 1.4
- base_rate: float32 [2048], P('scen'), may hold values from 0.01 to 0.06
- rate_moves: float32 [3, 2048], P(None, 'scen'), may hold values from -0.012 to 0.012
- guarantee: float32 [256], replicated, may hold values from 0 to 0.035
- spread: float32 [256], replicated, may hold values from 0 to 0.03
- start_rate: float32 [2048, 256], P('scen'), may hold values from 0 to 0.05
Outputs:
- occupancy: float32 [8, 2048, 16384], P(None, 'scen', 'mp')
- account_value: float32 [2048, 16384], P('scen', 'mp')
- credited_pct: float32 [2048, 256], P('scen', 'mp')
- outflow_value: float32 [256], P('mp')
All inputs are finite; a program needn't handle non-finite values.
Results may differ from a plain program's by a relative error of at most 0.0003.
Values sent between devices are 32-bit elements; how exact they have to be, the bound alone decides.
A program may use at most 128 MiB of HBM per device.

v0:
```python
import jax
import jax.numpy as jnp
from jax import lax
from jax.sharding import PartitionSpec as P

EXACT = lax.Precision.HIGHEST
STAY_WEIGHT = 40.0
LAPSE_SLOPE = 30.0
LIQUID_CHARGE = 0.5


def discount(rate_now, date_index, term_count):
    horizon = jnp.arange(term_count, dtype=jnp.int32)
    tenor = (horizon - date_index + 1).astype(jnp.float32) / 12.0
    live = horizon >= date_index
    factor = jnp.exp(-rate_now[:, None] * tenor[None, :])
    return jnp.where(live[None, :], factor, jnp.zeros_like(factor))


def new_rates(held_value, later_value, group_flows, credited, guarantee, spread):
    earned = 12.0 * (later_value - held_value) / held_value
    return jnp.maximum(
        guarantee[None, :],
        0.5 * credited
        + 0.5 * (earned - spread[None, :])
        - LIQUID_CHARGE * group_flows / held_value,
    )


def body(
    group_id,
    issue_state,
    account_start,
    transition,
    lapse_base,
    benefit,
    bond_block,
    bond_flows,
    bond_target,
    base_rate,
    rate_moves,
    guarantee,
    spread,
    start_rate,
):
    group_count = transition.shape[0]
    state_count = transition.shape[1]
    scen_dev = base_rate.shape[0]
    scen_all = scen_dev * lax.axis_size("scen")
    month_count = rate_moves.shape[0]
    term_count = bond_flows.shape[1]
    owned_count = group_count // lax.axis_size("mp")
    first_group = lax.axis_index("mp") * owned_count
    labels = jnp.arange(group_count, dtype=jnp.int32)
    member = (group_id[:, None] == labels[None, :]).astype(jnp.float32)
    bond_member = (bond_block[:, 0][:, None] == labels[None, :]).astype(jnp.float32)
    stochastic = transition + STAY_WEIGHT * jnp.eye(state_count, dtype=jnp.float32)[None]
    stochastic = stochastic / jnp.sum(stochastic, axis=2, keepdims=True)
    point_moves = jnp.dot(
        member, stochastic.reshape(group_count, state_count * state_count), precision=EXACT
    ).T.reshape(state_count, state_count, -1)
    point_lapse = jnp.dot(member, lapse_base, precision=EXACT)
    rate_path = [base_rate]
    for step_month in range(month_count):
        rate_path.append(rate_path[-1] + rate_moves[step_month])
    states = jnp.arange(state_count, dtype=jnp.int32)
    start_mass = (issue_state[None, :] == states[:, None]).astype(jnp.float32)
    occupancy = jnp.broadcast_to(
        start_mass[:, None, :], (state_count, scen_dev, start_mass.shape[1])
    )
    account_value = jnp.broadcast_to(account_start[None, :], (scen_dev, account_start.shape[0]))
    credited = start_rate
    final_rate = lax.dynamic_slice_in_dim(start_rate, first_group, owned_count, 1)
    present = jnp.zeros((scen_dev, owned_count), jnp.float32)
    for step_month in range(month_count):
        point_rate = jnp.dot(credited, member.T, precision=EXACT)
        lapse_rate = (
            point_lapse[None, :]
            * 2.0
            * jax.nn.sigmoid(LAPSE_SLOPE * (rate_path[step_month][:, None] - point_rate))
        )
        lapsed_mass = occupancy[0] * lapse_rate
        kept_mass = jnp.concatenate([(occupancy[0] - lapsed_mass)[None], occupancy[1:]], axis=0)
        occupancy = jnp.einsum("scm,sum->ucm", kept_mass, point_moves, precision=EXACT)
        account_value = account_value * (1.0 + point_rate / 12.0)
        paid_share = jnp.einsum("u,ucm->cm", benefit, occupancy, precision=EXACT)
        outflow = account_value * (lapsed_mass + paid_share)
        group_flows = jnp.dot(outflow, member, precision=EXACT)
        date_list = [step_month, step_month + 1]
        raw_prices = jnp.stack(
            [
                jnp.dot(
                    discount(rate_path[date_index], date_index, term_count),
                    bond_flows.T,
                    precision=EXACT,
                )
                for date_index in date_list
            ]
        )
        totals = lax.psum(jnp.sum(raw_prices, axis=1), "scen")
        scaled = raw_prices * (bond_target[None, :] / (totals / scen_all))[:, None, :]
        held_value, later_assets = [
            jnp.dot(scaled[number], bond_member, precision=EXACT)
            for number in range(len(date_list))
        ]
        income = jnp.dot(bond_flows[:, step_month], bond_member, precision=EXACT)
        later_value = later_assets + income[None, :]
        stacked = jnp.stack([held_value, later_value, group_flows])
        summed_all = lax.psum(stacked, "mp")
        credited = new_rates(
            summed_all[0], summed_all[1], summed_all[2], credited, guarantee, spread
        )
        final_rate = lax.dynamic_slice_in_dim(credited, first_group, owned_count, 1)
        owned_flows = lax.dynamic_slice_in_dim(summed_all[2], first_group, owned_count, 1)
        present = (
            present
            + owned_flows * jnp.exp(-rate_path[step_month + 1] * (step_month + 1) / 12.0)[:, None]
        )
    outflow_value = lax.psum(jnp.sum(present, axis=0), "scen") / scen_all
    return (occupancy, account_value, 100.0 * final_rate, outflow_value)


def solution(mesh):
    placed = (
        P("mp"),
        P("mp"),
        P("mp"),
        P(),
        P(),
        P(),
        P("mp", None),
        P("mp", None),
        P("mp"),
        P("scen"),
        P(None, "scen"),
        P(),
        P(),
        P("scen", None),
    )
    return jax.shard_map(
        body,
        mesh=mesh,
        in_specs=placed,
        out_specs=(P(None, "scen", "mp"), P("scen", "mp"), P("scen", "mp"), P("mp")),
        check_vma=False,
    )
```

profile of v0, /device:TPU:0, one launch (start us, length us, event | category | flops | bytes accessed | tf_op | source)
XLA Modules:
  0.0 763.3 jit_solution(9830515649147443233)
XLA Ops:
  7.3 0.7 compare_convert_fusion
  8.1 1.2 multiply_exponential_fusion.2
  9.3 1.2 multiply_exponential_fusion.1
  10.5 1.2 multiply_exponential_fusion
  11.7 1.3 fusion.47
  13.1 4.0 slice_reduce_fusion
  17.3 0.7 fusion.49
  18.0 1.0 copy.58
  19.0 0.9 fusion.14
  20.0 2.9 convolution_bitcast_fusion.3
  22.9 2.8 convolution_bitcast_fusion
  25.7 2.8 convolution_bitcast_fusion.1
  28.6 2.8 convolution_bitcast_fusion.2
  31.4 0.7 fusion.18
  32.5 79.6 %all-reduce = (f32[2,2560]{1,0:T(2,128)S(1)}, f32[2,2560]{1,0:T(2,128)S(1)}, f32[2,2560]{1,0:T(2,128)S(1)}) all-reduce(f32[2,2560]{1,0:T(2,128)S(1)} %get-tuple-element.17, f32[2,2560]{1,0:T(2,128)S(1)} %get-tuple-element.16, f32[2,2560]{1,0:T(2,128)S(1)} %get-tuple-element.15), channel_id=1, replica_groups=mesh['mp'=16,'scen'=16] {'scen'}, use_global_device_ids=true, to_apply=%region_2.3 | all-reduce | flops 15360 | bytes 122880 | tf_op jit(solution)/shard_map/psum | solution.py:100
  112.1 5.7 fusion.17
  117.8 1.2 fusion.35
  119.0 1.2 fusion.39
  120.2 2.7 copy.43
  122.9 0.7 bitcast_subtract_fusion
  123.9 1.1 broadcast_in_dim.44
  125.1 0.9 copy-done.3
  126.0 7.7 %fusion = f32[1024,8,128]{2,1,0:T(8,128)S(1)} fusion(f32[8,8,1024]{0,1,2:T(8,128)S(1)} %copy-done.3, f32[7,128,1024]{1,0,2:T(8,128)S(1)} %broadcast_in_dim.44, f32[1,128,1024]{1,0,2:T(1,128)S(1)} %bitcast.264), kind=kOutput, calls=%fused_computation | convolution fusion | flops 101711872 | bytes 8650752 | tf_op jit(solution)/shard_map/scm,sum->ucm/dot_general | solution.py:84
  133.7 0.8 multiply_reduce_fusion.1
  134.6 1.2 convolution_bitcast_fusion.6
  135.8 0.8 pad_maximum_fusion.5
  136.9 3.1 copy.72
  140.0 0.7 reshape.141
  140.7 1.2 fusion.37
  141.9 1.9 fusion.36
  143.8 2.0 slice.129
  145.9 0.9 fusion.11
  146.8 1.8 fusion.41
  148.6 162.8 %all-reduce.5.cloned.1.call-done = f32[3,128,256]{2,1,0:T(8,128)} async-done(((f32[3,128,256]{2,1,0:T(8,128)}), f32[3,128,256]{2,1,0:T(8,128)}) %all-reduce.5.cloned.1.call-update) | async-done | bytes 393232 | tf_op jit(solution)/shard_map/psum | solution.py:109
  311.4 1.1 fusion.93
  312.5 0.6 fusion.45
  313.1 1.3 subtract_bitcast_fusion.1
  314.4 2.5 pad_maximum_fusion
  316.9 0.8 copy-done.4
  317.7 9.7 %fusion.6 = f32[1024,8,128]{2,1,0:T(8,128)S(1)} fusion(f32[8,8,1024]{0,1,2:T(8,128)S(1)} %copy-done.4, f32[8,128,1024]{1,2,0:T(8,128)S(1)} %pad_maximum_fusion), kind=kOutput, calls=%fused_computation.11 | convolution fusion | flops 100663296 | bytes 8650752 | tf_op jit(solution)/shard_map/scm,sum->ucm/dot_general | solution.py:84
  327.5 0.8 multiply_reduce_fusion
  328.9 2.4 convolution_bitcast_fusion.5
  331.3 0.8 pad_maximum_fusion.6
  332.1 1.7 fusion.8
  333.8 1.9 fusion.43
  335.7 3.0 copy.71
  338.7 1.9 copy-done.10
  340.6 2.0 slice.136
  342.7 167.4 %all-reduce.7.cloned.1.call-done = f32[3,128,256]{2,1,0:T(8,128)} async-done(((f32[3,128,256]{2,1,0:T(8,128)}), f32[3,128,256]{2,1,0:T(8,128)}) %all-reduce.7.cloned.1.call-update) | async-done | bytes 393232 | tf_op jit(solution)/shard_map/psum | solution.py:109
  510.1 1.2 fusion.94
  511.3 0.6 fusion.44
  512.0 1.4 add_multiply_fusion
  513.7 1.9 copy-done.5
  515.6 9.7 %fusion.23 = f32[8,128,1024]{1,0,2:T(8,128)S(1)} fusion(f32[8,8,1024]{0,1,2:T(8,128)S(1)} %copy-done.5, f32[8,128,1024]{1,2,0:T(8,128)S(1)} %pad_maximum_fusion.1), kind=kOutput, calls=%fused_computation.37 | convolution fusion | flops 100663296 | bytes 8650752 | tf_op jit(solution)/shard_map/scm,sum->ucm/dot_general | solution.py:84
  525.4 3.8 fusion.123
  529.2 2.0 convolution_bitcast_fusion.4
  531.1 0.8 pad_maximum_fusion.7
  532.1 1.0 copy.47
  533.1 5.4 copy.46
  538.6 171.5 %all-reduce.9.cloned.1.call-done = f32[3,128,256]{2,1,0:T(8,128)} async-done(((f32[3,128,256]{2,1,0:T(8,128)}), f32[3,128,256]{2,1,0:T(8,128)}) %all-reduce.9.cloned.1.call-update) | async-done | bytes 393232 | tf_op jit(solution)/shard_map/psum | solution.py:109
  710.0 1.0 fusion.67
  711.0 1.0 fusion.134
  712.1 0.7 copy.48
  713.0 42.7 %psum.55 = f32[16]{0:T(128)S(1)} all-reduce(f32[16]{0:T(128)S(1)} %fusion.102), channel_id=1, replica_groups=mesh['mp'=16,'scen'=16] {'scen'}, use_global_device_ids=true, to_apply=%region_11.12 | all-reduce | flops 16 | bytes 128 | tf_op jit(solution)/shard_map/psum | solution.py:119
  (114 shorter events, 3.3 us)
Async XLA Ops:
  7.2 4.6 copy-start
  7.2 10.1 %copy-start.24 = (s32[1024]{0:T(1024)S(1)}, s32[1024]{0:T(1024)}, u32[]{:S(2)}) copy-start(s32[1024]{0:T(1024)} %param.14) | copy-start | bytes 12292
  7.2 9.9 %copy-start.23 = (f32[256,8,8]{0,2,1:T(8,128)S(1)}, f32[256,8,8]{0,2,1:T(8,128)}, u32[]{:S(2)}) copy-start(f32[256,8,8]{0,2,1:T(8,128)} %param.17) | copy-start | bytes 196612
  7.2 304.2 %all-reduce.5.cloned.1.call-start = ((), (), s32[]{:S(2)}) async-start(), calls=%async_computation | async-start | bytes 786432 | tf_op jit(solution)/shard_map/psum | solution.py:109
  10.5 8.5 %copy-start.30 = (f32[128]{0:T(128)}, f32[128]{0:T(128)S(1)}, u32[]{:S(2)}) copy-start(f32[128]{0:T(128)S(1)} %get-tuple-element.24) | copy-start | bytes 1540
  13.0 6.0 copy-start.28
  13.1 6.9 copy-start.2
  19.0 121.7 %copy-start.26 = (s32[2560]{0:T(1024)}, s32[2560]{0:T(1024)S(1)}, u32[]{:S(2)}) copy-start(s32[2560]{0:T(1024)S(1)} %reduce.2) | copy-start | bytes 30724
  22.9 8.6 %copy-start.12 = (f32[1,128,2560]{2,1,0:T(8,128)}, f32[1,128,2560]{2,1,0:T(8,128)S(1)}, u32[]{:S(2)}) copy-start(f32[1,128,2560]{2,1,0:T(8,128)S(1)} %convolution_bitcast_fusion.3) | copy-start | bytes 3932164
  25.7 5.7 copy-start.13
  28.6 3.6 copy-start.14
  31.4 1.1 copy-start.15
  31.4 80.7 %copy-start.25 = (f32[2560]{0:T(1024)S(1)}, f32[2560]{0:T(1024)}, u32[]{:S(2)}) copy-start(f32[2560]{0:T(1024)} %param.22) | copy-start | bytes 30724
  120.2 2.7 copy-start.21
  120.2 2.7 copy-start.42
  122.9 1.0 copy-start.17
  123.6 11.0 %copy-start.18 = (f32[1024,128]{1,0:T(8,128)}, f32[1024,128]{1,0:T(8,128)S(1)}, u32[]{:S(2)}) copy-start(f32[1024,128]{1,0:T(8,128)S(1)} %get-tuple-element.42) | copy-start | bytes 1572868
  123.6 2.4 copy-start.3
  126.0 7.7 %copy-start.29 = (f32[8]{0:T(128)S(1)}, f32[8]{0:T(128)}, u32[]{:S(2)}) copy-start(f32[8]{0:T(128)} %param.19) | copy-start | bytes 100
  133.7 2.1 copy-start.8
  133.7 0.9 copy-start.32
  136.6 373.4 %all-reduce.7.cloned.1.call-start = ((), (), s32[]{:S(2)}) async-start(), calls=%async_computation.1 | async-start | bytes 786432 | tf_op jit(solution)/shard_map/psum | solution.py:109
  136.9 5.0 copy-start.16
  140.0 5.8 copy-start.9
  143.8 2.1 copy-start.27
  143.8 167.6 %copy-start.35 = (f32[256]{0:T(256)S(1)}, f32[256]{0:T(256)}, u32[]{:S(2)}) copy-start(f32[256]{0:T(256)} %param.25) | copy-start | bytes 3076
  143.8 167.6 %copy-start.37 = (f32[256]{0:T(256)S(1)}, f32[256]{0:T(256)}, u32[]{:S(2)}) copy-start(f32[256]{0:T(256)} %param.26) | copy-start | bytes 3076
  314.4 3.3 copy-start.4
  327.4 3.8 copy-start.7
  327.4 1.4 copy-start.19
  327.4 1.4 copy-start.33
  328.9 2.4 copy-start.22
  332.1 377.9 %all-reduce.9.cloned.1.call-start = ((), (), s32[]{:S(2)}) async-start(), calls=%async_computation.2 | async-start | bytes 786432 | tf_op jit(solution)/shard_map/psum | solution.py:109
  338.7 2.0 copy-start.10
  340.6 169.5 %copy-start.36 = (f32[256]{0:T(256)S(1)}, f32[256]{0:T(256)}, u32[]{:S(2)}) copy-start(f32[256]{0:T(256)} %param.25) | copy-start | bytes 3076
  340.6 169.5 %copy-start.38 = (f32[256]{0:T(256)S(1)}, f32[256]{0:T(256)}, u32[]{:S(2)}) copy-start(f32[256]{0:T(256)} %param.26) | copy-start | bytes 3076
  340.6 171.4 %copy-start.20 = (f32[1024,128]{1,0:T(8,128)S(1)}, f32[1024,128]{1,0:T(8,128)}, u32[]{:S(2)}) copy-start(f32[1024,128]{1,0:T(8,128)} %copy-done.18) | copy-start | bytes 1572868
  340.6 171.4 %copy-start.31 = (f32[128]{0:T(128)S(1)}, f32[128]{0:T(128)}, u32[]{:S(2)}) copy-start(f32[128]{0:T(128)} %copy-done.30) | copy-start | bytes 1540
  340.6 171.4 %copy-start.34 = (f32[1024]{0:T(1024)S(1)}, f32[1024]{0:T(1024)}, u32[]{:S(2)}) copy-start(f32[1024]{0:T(1024)} %param.16) | copy-start | bytes 12292
  510.1 3.3 copy-start.11
  513.4 2.2 copy-start.5
  525.4 5.8 copy-start.6
  533.1 179.7 %slice-start = ((f32[3,128,256]{2,1,0:T(8,128)}), f32[1,128,256]{2,1,0:T(8,128)S(1)}, s32[]{:S(2)}) async-start(f32[3,128,256]{2,1,0:T(8,128)} %all-reduce.5.cloned.1.call-done), calls=%async_computation.3 | async-start | bytes 262144 | tf_op jit(solution)/shard_map/slice | solution.py:111
  533.1 179.7 %slice-start.1 = ((f32[3,128,256]{2,1,0:T(8,128)}), f32[1,128,256]{2,1,0:T(8,128)S(1)}, s32[]{:S(2)}) async-start(f32[3,128,256]{2,1,0:T(8,128)} %all-reduce.7.cloned.1.call-done), calls=%async_computation.4 | async-start | bytes 262144 | tf_op jit(solution)/shard_map/slice | solution.py:111
  533.1 179.7 %copy-start.39 = (f32[128]{0:T(128)S(1)}, f32[128]{0:T(128)}, u32[]{:S(2)}) copy-start(f32[128]{0:T(128)} %get-tuple-element.21) | copy-start | bytes 1540
  533.1 179.7 %copy-start.40 = (f32[128]{0:T(128)S(1)}, f32[128]{0:T(128)}, u32[]{:S(2)}) copy-start(f32[128]{0:T(128)} %get-tuple-element.23) | copy-start | bytes 1540
  533.1 179.7 %copy-start.41 = (f32[128]{0:T(128)S(1)}, f32[128]{0:T(128)}, u32[]{:S(2)}) copy-start(f32[128]{0:T(128)} %get-tuple-element.25) | copy-start | bytes 1540
  533.1 223.2 %copy-start.1 = (f32[256]{0:T(256)S(1)}, f32[256]{0:T(256)}, u32[]{:S(2)}) copy-start(f32[256]{0:T(256)} %param.18) | copy-start | bytes 3076
Sparse Core Ops, SparseCore 0:
  136.8 174.6 all-reduce.4
  332.2 177.8 all-reduce.6
  532.1 177.8 all-reduce.8
where the time goes:
time: 773 us; the launch traced here: 763 us
  waiting for transfers between devices  502 us (65%)
  blocking collectives  122 us (16%)
  matrix products  64.4 us (8%)
  local copies, waits for them, and re-layouts  34 us (4%)
  other arithmetic  25.7 us (3%)
  between operations  14.9 us (2%)
    psum x3, waiting for transfers between devices, body(): summed_all = lax.psum(stacked, 'mp')  502 us
    psum x1, blocking collectives, body(): totals = lax.psum(jnp.sum(raw_prices, axis=1), 'scen')  79.6 us
    psum x1, blocking collectives, body(): outflow_value = lax.psum(jnp.sum(present, axis=0), 'scen') / scen_all  42.7 us
    dot_general x3, matrix products, body(): jnp.einsum('scm,sum->ucm', kept_mass, point_moves, precision=EXACT)  27.2 us
  transfers between devices with their start and end apart: 3, of which 3 were waited for; matrix products, arithmetic and copies ran while one was open for 4% of the time, Pallas kernels for 0%

commit v1 on v0

v1 whole, which is shorter than its diff:
```python
import jax
import jax.numpy as jnp
from jax import lax
from jax.sharding import PartitionSpec as P

EXACT = lax.Precision.HIGHEST
STAY_WEIGHT = 40.0
LAPSE_SLOPE = 30.0
LIQUID_CHARGE = 0.5


def dot(a, b):
    return jnp.dot(a, b, precision=EXACT)


def body(
    group_id,
    issue_state,
    account_start,
    transition,
    lapse_base,
    benefit,
    bond_block,
    bond_flows,
    bond_target,
    base_rate,
    rate_moves,
    guarantee,
    spread,
    start_rate,
):
    group_count, state_count = transition.shape[:2]
    scen_dev = base_rate.shape[0]
    scen_axis, mp_axis = lax.axis_size("scen"), lax.axis_size("mp")
    scen_all = scen_dev * scen_axis
    month_count = rate_moves.shape[0]
    term_count = bond_flows.shape[1]
    owned = group_count // mp_axis
    first_group = lax.axis_index("mp") * owned
    term_dev = term_count // scen_axis
    labels = jnp.arange(group_count, dtype=jnp.int32)

    def own_rows(array):
        return lax.dynamic_slice_in_dim(array, first_group, owned, 0)

    rate_path = [base_rate]
    for month in range(month_count):
        rate_path.append(rate_path[-1] + rate_moves[month])
    horizon = jnp.arange(term_count, dtype=jnp.int32)
    discounts = []
    for date in range(month_count + 1):
        tenor = (horizon - date + 1).astype(jnp.float32) / 12.0
        factor = jnp.exp(-tenor[:, None] * rate_path[date][None, :])
        discounts.append(jnp.where((horizon >= date)[:, None], factor, 0.0))
    discounts = jnp.stack(discounts)
    mean_discount = lax.psum(jnp.sum(discounts, axis=2), "scen") / scen_all

    mean_price = dot(mean_discount, bond_flows.T)
    weight = bond_target[None, :] / mean_price
    bond_member = (bond_block[:, 0][None, :] == labels[:, None]).astype(jnp.float32)
    first_term = lax.axis_index("scen") * term_dev
    flows_dev = lax.dynamic_slice_in_dim(bond_flows.T, first_term, term_dev, 0)
    scaled = (weight[:, None, :] * flows_dev[None, :, :]).reshape(-1, flows_dev.shape[1])
    worth = dot(bond_member, scaled.T)
    income = dot(bond_member, bond_flows[:, :month_count])

    member = (group_id[None, :] == labels[:, None]).astype(jnp.float32)
    states = jnp.arange(state_count, dtype=jnp.int32)
    start_mass = (issue_state[None, :] == states[:, None]).astype(jnp.float32)
    accounts = dot(member, (start_mass * account_start[None, :]).T)
    summed = lax.psum_scatter(
        jnp.concatenate([worth, income, accounts], axis=1), "mp", scatter_dimension=0, tiled=True
    )
    width = worth.shape[1]
    income, accounts = summed[:, width : width + month_count], summed[:, width + month_count :]
    worth = lax.all_gather(summed[:, :width].reshape(owned, month_count + 1, term_dev), "scen", axis=2, tiled=True)
    assets = [dot(worth[:, date], discounts[date]) for date in range(month_count + 1)]

    move = transition + STAY_WEIGHT * jnp.eye(state_count, dtype=jnp.float32)[None]
    move = move / jnp.sum(move, axis=2, keepdims=True)
    powers = [move]
    for _ in range(month_count - 1):
        powers.append(jnp.sum(powers[-1][:, :, :, None] * move[:, None, :, :], axis=2))

    own_powers = [own_rows(power) for power in powers]
    own_starts = [accounts[:, 0]] + [jnp.sum(accounts * power[:, :, 0], axis=1) for power in own_powers]
    own_pays = [jnp.sum(power * benefit[None, None, :], axis=2) for power in own_powers]
    own_start_pays = [jnp.sum(accounts * pay, axis=1) for pay in own_pays]

    credited = own_rows(start_rate.T)
    path = [credited]
    lapse_own, guarantee_own, spread_own = own_rows(lapse_base), own_rows(guarantee), own_rows(spread)
    growth = jnp.ones_like(credited)
    lapses = []
    present = jnp.zeros_like(credited)
    for month in range(month_count):
        factor = lapse_own[:, None] * 2.0 * jax.nn.sigmoid(LAPSE_SLOPE * (rate_path[month][None, :] - credited))
        first = own_starts[month][:, None]
        for lag, lapse in enumerate(reversed(lapses)):
            first = first - lapse * own_powers[lag][:, 0, 0][:, None]
        lapses.append(first * factor)
        growth = growth * (1.0 + credited / 12.0)
        paid = own_start_pays[month][:, None]
        for lag, lapse in enumerate(reversed(lapses)):
            paid = paid - lapse * own_pays[lag][:, 0][:, None]
        flows = growth * (lapses[-1] + paid)
        held = assets[month]
        later = assets[month + 1] + income[:, month][:, None]
        earned = 12.0 * (later - held) / held
        credited = jnp.maximum(
            guarantee_own[:, None],
            0.5 * credited + 0.5 * (earned - spread_own[:, None]) - LIQUID_CHARGE * flows / held,
        )
        path.append(credited)
        present = present + flows * jnp.exp(-rate_path[month + 1] * (month + 1) / 12.0)[None, :]
    outflow_value = lax.psum(jnp.sum(present, axis=1), "scen") / scen_all

    others = lax.all_gather(jnp.stack(path[1:month_count]), "mp", axis=1, tiled=True)
    rates = [start_rate] + [others[month].T for month in range(month_count - 1)]
    growth = jnp.ones_like(start_rate)
    tables = []
    for month in range(month_count):
        tables.append(
            lapse_base[None, :]
            * 2.0
            * jax.nn.sigmoid(LAPSE_SLOPE * (rate_path[month][:, None] - rates[month]))
        )
        growth = growth * (1.0 + rates[month] / 12.0)
    points = dot(jnp.concatenate(tables + [growth]), member).reshape(month_count + 1, scen_dev, -1)
    point_powers = [
        dot(power.transpose(1, 2, 0).reshape(-1, group_count), member).reshape(state_count, state_count, -1)
        for power in powers
    ]
    own_state = [jnp.sum(start_mass[:, None, :] * power, axis=0) for power in point_powers]
    lapses = []
    for month in range(month_count):
        first = (start_mass[0] if month == 0 else own_state[month - 1][0])[None, :]
        for lag, lapse in enumerate(reversed(lapses)):
            first = first - lapse * point_powers[lag][0, 0][None, :]
        lapses.append(first * points[month])
    occupancy = own_state[-1][:, None, :]
    for lag, lapse in enumerate(reversed(lapses)):
        occupancy = occupancy - lapse[None] * point_powers[lag][0][:, None, :]
    account_value = account_start[None, :] * points[month_count]
    return (occupancy, account_value, 100.0 * credited.T, outflow_value)


def solution(mesh):
    placed = (
        P("mp"),
        P("mp"),
        P("mp"),
        P(),
        P(),
        P(),
        P("mp", None),
        P("mp", None),
        P("mp"),
        P("scen"),
        P(None, "scen"),
        P(),
        P(),
        P("scen", None),
    )
    return jax.shard_map(
        body,
        mesh=mesh,
        in_specs=placed,
        out_specs=(P(None, "scen", "mp"), P("scen", "mp"), P("scen", "mp"), P("mp")),
        check_vma=False,
    )
```

time: 773 us -> 271 us (0.35)
  the two profiles are of different devices: /device:TPU:0 before, /device:TPU:8 now
where the time goes in v1:
time: 271 us; the launch traced here: 270 us
  blocking collectives  151 us (56%)
  waiting for transfers between devices  75.1 us (28%)
  between operations  14.4 us (5%)
  matrix products  12.1 us (4%)
  other arithmetic  9.22 us (3%)
  local copies, waits for them, and re-layouts  8.69 us (3%)
    unnamed x2, waiting for transfers between devices  75.1 us
    psum x1, blocking collectives, body(): outflow_value = lax.psum(jnp.sum(present, axis=1), 'scen') / scen_all  42.4 us
    all_gather x1, blocking collectives, body(): lax.all_gather(summed[:, :width].reshape(owned, month_count + 1, term_dev...  40.2 us
    psum x1, blocking collectives, body(): mean_discount = lax.psum(jnp.sum(discounts, axis=2), 'scen') / scen_all  40.1 us
    all_gather x1, blocking collectives, body(): lax.all_gather(jnp.stack(path[1:month_count]), 'mp', axis=1, tiled=True)  27.9 us
    dot_general x12, matrix products, dot(): return jnp.dot(a, b, precision=EXACT)  12.1 us
  transfers between devices with their start and end apart: 1, of which 1 were waited for; matrix products, arithmetic and copies ran while one was open for 1% of the time, Pallas kernels for 0%

profile of v1, /device:TPU:8, one launch (start us, length us, event | category | flops | bytes accessed | tf_op | source)
XLA Modules:
  0.0 270.3 jit_solution(884982691692637436)
XLA Ops:
  7.2 0.0 reduce-scatter.4.cloned.1.call-start
  7.3 0.7 multiply_exponential_fusion.3
  8.0 0.7 multiply_exponential_fusion.2
  8.7 0.7 multiply_exponential_fusion.1
  9.4 0.7 reduce
  10.1 0.8 exponential_select_fusion.2
  11.0 0.2 exponential_select_fusion
  11.2 0.2 maximum_reduce_fusion
  11.4 40.1 %psum.14 = f32[4,256]{1,0:T(4,128)S(1)} all-reduce(f32[4,256]{1,0:T(4,128)S(1)} %maximum_reduce_fusion), channel_id=1, replica_groups=mesh['mp'=16,'scen'=16] {'scen'}, use_global_device_ids=true, to_apply=%region_7.8 | all-reduce | flops 1024 | bytes 8192 | tf_op jit(solution)/shard_map/psum | solution.py:56
  51.5 0.0 copy-start.5
  51.5 2.7 %fusion = f32[256,3]{0,1:T(4,128)S(1)} fusion(f32[2560,256]{1,0:T(8,128)} %param.21, s32[2560]{0:T(1024)S(1)} %reduce), kind=kOutput, calls=%fused_computation.3 | convolution fusion | flops 24248320 | bytes 1324032 | tf_op jit(solution)/shard_map/dot_general | solution.py:13
  54.3 2.8 %dynamic-slice_bitcast_fusion = f32[16,2560]{0,1:T(8,128)} fusion(f32[2560,256]{1,0:T(8,128)} %param.21, s32[]{:T(128)S(6)} %select_n.55), kind=kLoop, calls=%fused_computation.6 | loop fusion | bytes 327684 | tf_op jit(solution)/shard_map/dynamic_slice | solution.py:62
  57.1 1.7 copy.42
  58.8 0.0 copy-done.5
  58.8 0.0 copy-start.1
  58.8 0.0 copy-start.9
  58.8 2.2 convolution_divide_fusion
  61.1 0.0 copy-start.10
  61.1 0.0 copy-start.11
  61.1 0.0 copy-start.12
  61.1 0.0 copy-start.3
  61.2 0.0 copy-start.6
  61.2 1.5 fusion.1
  62.7 0.6 fusion.15
  63.3 0.8 copy.44
  64.0 0.0 reduce-scatter.4.cloned.1.call-update
  64.1 0.0 copy-start.2
  64.1 0.1 add_reduce_fusion
  64.2 0.1 add_divide_fusion
  64.3 0.5 fusion.16
  64.9 0.5 fusion.17
  65.4 0.1 fusion.96
  65.5 0.0 copy-done.10
  65.5 0.1 multiply_reduce_fusion.4
  65.6 0.5 fusion.31
  66.1 0.1 dynamic-slice_multiply_fusion
  66.2 0.0 copy-done.11
  66.2 0.1 dynamic_slice.26
  66.3 0.1 dynamic_slice.30
  66.4 0.1 copy.40
  66.5 0.1 constant_dynamic-slice_fusion.1
  66.6 75.1 %reduce-scatter.4.cloned.1.call-done = f32[16,75]{1,0:T(8,128)} async-done(((f32[256,75]{1,0:T(8,128)}), f32[16,75]{1,0:T(8,128)}) %reduce-scatter.4.cloned.1.call-update) | async-done | bytes 4816
  141.7 0.8 copy.46
  142.5 40.2 %all_gather.6 = f32[16,4,256]{0,2,1:T(8,128)S(1)} all-gather(f32[16,4,16]{0,2,1:T(8,128)S(1)} %bitcast.210), channel_id=1, replica_groups=mesh['mp'=16,'scen'=16] {'scen'}, dimensions={2}, use_global_device_ids=true | all-gather | bytes 69632 | tf_op jit(solution)/shard_map/all_gather | solution.py:76
  182.7 0.4 fusion.32
  183.2 0.4 fusion.33
  183.6 0.8 slice.165
  184.4 0.1 copy.49
  184.5 0.9 fusion.105
  185.4 0.1 copy.50
  185.5 0.1 copy.48
  185.5 0.1 copy.47
  185.7 0.6 add_reduce_fusion.1
  186.3 27.9 %all_gather.7 = f32[2,256,128]{2,1,0:T(8,128)S(1)} all-gather(f32[2,16,128]{2,1,0:T(8,128)S(1)} %pad_maximum_fusion.1), channel_id=1, replica_groups=mesh['mp'=16,'scen'=16] {'mp'}, dimensions={1}, use_global_device_ids=true | all-gather | bytes 278528 | tf_op jit(solution)/shard_map/all_gather | solution.py:118
  214.2 0.1 divide_multiply_fusion
  214.3 0.0 slice-start
  214.3 0.1 multiply_bitcast_fusion.1
  214.4 0.1 copy.51
  214.5 42.4 %psum.15 = f32[16]{0:T(128)S(1)} all-reduce(f32[16]{0:T(128)S(1)} %get-tuple-element.15), channel_id=1, replica_groups=mesh['mp'=16,'scen'=16] {'scen'}, use_global_device_ids=true, to_apply=%region_18.19 | all-reduce | flops 16 | bytes 128 | tf_op jit(solution)/shard_map/psum | solution.py:116
  256.9 0.5 broadcast_multiply_fusion.2
  257.4 1.1 fusion.13
  258.5 1.1 fusion.14
  259.6 1.0 slice_multiply_fusion.1
  260.6 2.8 %multiply_subtract_fusion = f32[8,128,1024]{2,1,0:T(8,128)} fusion(f32[8,1024]{1,0:T(8,128)S(1)} %slice.177, f32[128,1024]{1,0:T(8,128)S(1)} %get-tuple-element.26, f32[8,1024]{1,0:T(8,128)S(1)} %slice.176, f32[128,1024]{1,0:T(8,128)S(1)} %get-tuple-element.25, f32[8,1024]{1,0:T(8,128)S(1)} %slice.175, f32[128,1024]{1,0:T(8,128)S(1)} %get-tuple-element.24, ...), kind=kLoop, calls=%fused_computation | loop fusion | flops 6291456 | bytes 5898240 | tf_op jit(solution)/shard_map/sub | solution.py:143
  (40 shorter events, 0.3 us)
Async XLA Ops:
  7.2 134.6 %reduce-scatter.4.cloned.1.call-start = ((), (), s32[]{:S(2)}) async-start(), calls=%async_computation.1 | async-start | bytes 139264
  51.5 7.3 %copy-start = (f32[2560,256]{1,0:T(8,128)S(1)}, f32[2560,256]{1,0:T(8,128)}, u32[]{:S(2)}) copy-start(f32[2560,256]{1,0:T(8,128)} %param.21) | copy-start | bytes 7864324
  51.5 7.3 %copy-start.5 = (f32[2560]{0:T(1024)S(1)}, f32[2560]{0:T(1024)}, u32[]{:S(2)}) copy-start(f32[2560]{0:T(1024)} %param.22) | copy-start | bytes 30724
  57.1 5.6 %copy-start.4 = (s32[1024]{0:T(1024)S(1)}, s32[1024]{0:T(1024)}, u32[]{:S(2)}) copy-start(s32[1024]{0:T(1024)} %param.14) | copy-start | bytes 12292
  57.1 5.6 %copy-start.7 = (s32[1024]{0:T(1024)S(1)}, s32[1024]{0:T(1024)}, u32[]{:S(2)}) copy-start(s32[1024]{0:T(1024)} %param.15) | copy-start | bytes 12292
  57.1 5.6 %copy-start.8 = (f32[1024]{0:T(1024)S(1)}, f32[1024]{0:T(1024)}, u32[]{:S(2)}) copy-start(f32[1024]{0:T(1024)} %param.16) | copy-start | bytes 12292
  58.8 5.3 %copy-start.1 = (f32[256,8,8]{0,2,1:T(8,128)S(1)}, f32[256,8,8]{0,2,1:T(8,128)}, u32[]{:S(2)}) copy-start(f32[256,8,8]{0,2,1:T(8,128)} %param.17) | copy-start | bytes 196612
  58.8 6.6 %copy-start.9 = (f32[256]{0:T(256)S(1)}, f32[256]{0:T(256)}, u32[]{:S(2)}) copy-start(f32[256]{0:T(256)} %param.18) | copy-start | bytes 3076
  61.1 4.4 %copy-start.10 = (f32[8]{0:T(128)S(1)}, f32[8]{0:T(128)}, u32[]{:S(2)}) copy-start(f32[8]{0:T(128)} %param.19) | copy-start | bytes 100
  61.1 5.1 %copy-start.11 = (f32[256]{0:T(256)S(1)}, f32[256]{0:T(256)}, u32[]{:S(2)}) copy-start(f32[256]{0:T(256)} %param.25) | copy-start | bytes 3076
  61.1 5.2 %copy-start.12 = (f32[256]{0:T(256)S(1)}, f32[256]{0:T(256)}, u32[]{:S(2)}) copy-start(f32[256]{0:T(256)} %param.26) | copy-start | bytes 3076
  61.1 5.3 %copy-start.3 = (f32[128,256]{1,0:T(8,128)S(1)}, f32[128,256]{1,0:T(8,128)}, u32[]{:S(2)}) copy-start(f32[128,256]{1,0:T(8,128)} %param.27) | copy-start | bytes 393220
  61.2 122.0 %copy-start.6 = (f32[128]{0:T(128)S(1)}, f32[128]{0:T(128)}, u32[]{:S(2)}) copy-start(f32[128]{0:T(128)} %param.23) | copy-start | bytes 1540
  64.1 150.1 %copy-start.2 = (f32[8,1024]{1,0:T(8,128)}, f32[8,1024]{1,0:T(8,128)S(1)}, u32[]{:S(2)}) copy-start(f32[8,1024]{1,0:T(8,128)S(1)} %fusion.64) | copy-start | bytes 98308
  214.3 45.3 %slice-start = ((f32[8,1024]{1,0:T(8,128)}), f32[1,1024]{1,0:T(1,128)S(1)}, s32[]{:S(2)}) async-start(f32[8,1024]{1,0:T(8,128)} %copy-done.2), calls=%async_computation.2 | async-start | bytes 8192 | tf_op jit(solution)/shard_map/slice | solution.py:137
Sparse Core Ops, SparseCore 0:
  64.2 77.5 reduce-scatter.3

commit v2 on v0

v2 whole, which is shorter than its diff:
```python
import functools

import jax
import jax.numpy as jnp
from jax import lax
from jax.experimental import pallas as pl
from jax.experimental.pallas import tpu as pltpu
from jax.sharding import PartitionSpec as P

MESH = pl.DeviceIdType.MESH
EXACT = lax.Precision.HIGHEST
F32, BF16 = jnp.float32, jnp.bfloat16
STAY_WEIGHT = 40.0
LAPSE_SLOPE = 30.0
LIQUID_CHARGE = 0.5

S = 8
PG = 256
K = 256
DATES = 4
MONTHS = 3
C = 128
M = 1024
B = 2560
TILE = 256
MP = 16
SC = 16
SCEN = C * SC
KD = K // SC
GQ = 2 * PG // MP
VMEM_LIMIT = 48 * 1024 * 1024

NT = (((1,), (1,)), ((), ()))
NN = (((1,), (0,)), ((), ()))


def dot(a, b, dims, precision=None):
    return lax.dot_general(a, b, dims, precision=precision, preferred_element_type=F32)


def parts(x, count):
    found = []
    for _ in range(count):
        found.append(x.astype(BF16))
        x = x - found[-1].astype(F32)
    return found


def stack_parts(x, count, rows):
    found = parts(x, count)
    pieces = [piece.astype(F32) for piece in found]
    rest = rows - count * x.shape[0]
    if rest:
        pieces.append(jnp.zeros((rest, x.shape[1]), F32))
    return jnp.concatenate(pieces, axis=0).astype(BF16)


def iota(shape, axis):
    return lax.broadcasted_iota(jnp.int32, shape, axis)


def group_at(place):
    block = place // 16
    return (block // 4 * 4 + block % 2 * 2 + block // 2 % 2) * 16 + place % 16


def swap_blocks(rows):
    block = iota(rows.shape, 1) // 16 % 4
    width = rows.shape[1]
    up = pltpu.roll(rows, width - 16, 1)
    down = pltpu.roll(rows, 16, 1)
    return jnp.where(block == 1, up, jnp.where(block == 2, down, rows))


def discounts(rates, date):
    horizon = iota((K, C), 0)
    tenor = (horizon - date + 1).astype(F32) / 12.0
    factor = jnp.exp(-tenor * rates[date : date + 1, :])
    return jnp.where(horizon >= date, factor, 0.0) if date else factor


def exchange_kernel(
    group_ref,
    state_ref,
    account_ref,
    transition_ref,
    rows_ref,
    benefit_ref,
    block_ref,
    flows_hbm,
    target_ref,
    base_ref,
    moves_ref,
    start_ref,
    rho_ref,
    pre_ref,
    table_ref,
    credited_ref,
    value_ref,
    path_ref,
    flows_ref,
    flow_parts,
    chosen_ref,
    bond_ref,
    point_ref,
    disc_ref,
    cols_ref,
    first_ref,
    a_src,
    a_buf,
    e_src,
    e_buf,
    b_src,
    b_buf,
    c_buf,
    d_buf,
    f_src,
    f_buf,
    load_sem,
    a_send,
    a_recv,
    e_send,
    e_recv,
    b_send,
    b_recv,
    c_send,
    c_recv,
    d_send,
    d_recv,
    f_send,
    f_recv,
):
    mp, sc = lax.axis_index("mp"), lax.axis_index("scen")
    x, zh, core = mp // 4, mp // 2 % 2, mp % 2
    own = x * 2 + core
    zl, y = sc // 4, sc % 4

    def mp_index(dx, dz, dc):
        return (x + dx) % 4 * 4 + (zh + dz) % 2 * 2 + (core + dc) % 2

    mp_peers = [
        mp_index(dx, dz, dc) for dz in (1, 0) for dx in (2, 1, 3, 0) for dc in (0, 1) if (dx, dz, dc) != (0, 0, 0)
    ]
    near_peers = [mp_index(dx, 0, dc) for dx in (2, 1, 3, 0) for dc in (0, 1) if (dx, dc) != (0, 0)]
    sc_peers = [
        (zl + dz) % 4 * 4 + (y + dy) % 4 for dz in (2, 1, 3, 0) for dy in (2, 1, 3, 0) if (dz, dy) != (0, 0)
    ]

    barrier = pltpu.get_barrier_semaphore()
    for peer in mp_peers:
        pl.semaphore_signal(barrier, inc=1, device_id=(peer, sc), device_id_type=MESH)
    for peer in sc_peers:
        pl.semaphore_signal(barrier, inc=1, device_id=(mp, peer), device_id_type=MESH)
    load = pltpu.make_async_copy(flows_hbm, flows_ref, load_sem)
    load.start()

    def to_scen(src, dst, send, recv):
        return [
            pltpu.make_async_remote_copy(
                src_ref=src, dst_ref=dst, send_sem=send.at[n], recv_sem=recv.at[sc],
                device_id=(mp, peer), device_id_type=MESH,
            )
            for n, peer in enumerate(sc_peers)
        ]

    def from_scen(src, slot, send, recv):
        for n, peer in enumerate(sc_peers):
            pltpu.make_async_remote_copy(
                src_ref=src, dst_ref=slot(peer), send_sem=send.at[n], recv_sem=recv.at[peer],
                device_id=(mp, peer), device_id_type=MESH,
            ).wait_recv()

    def to_mp(src, dst, send, recv, peers, mark):
        return [
            pltpu.make_async_remote_copy(
                src_ref=src(peer), dst_ref=dst, send_sem=send.at[n], recv_sem=recv.at[mark],
                device_id=(peer, sc), device_id_type=MESH,
            )
            for n, peer in enumerate(peers)
        ]

    def from_mp(src, slot, send, recv, peers, mark):
        for n, peer in enumerate(peers):
            pltpu.make_async_remote_copy(
                src_ref=src(peer), dst_ref=slot(peer), send_sem=send.at[n], recv_sem=recv.at[mark(peer)],
                device_id=(peer, sc), device_id_type=MESH,
            ).wait_recv()

    def pair(index):
        return index // 4 * 2 + index % 2

    rates = [base_ref[...]]
    for month in range(MONTHS):
        rates.append(rates[-1] + moves_ref[month : month + 1, :])
    rates = jnp.concatenate(rates, axis=0)
    path_ref[...] = jnp.concatenate([rates, jnp.zeros_like(rates)], axis=0)
    ones = jnp.ones((16, C), BF16)
    sums = []
    for date in range(DATES):
        pieces = parts(discounts(rates, date), 3)
        total = jnp.zeros((16, K), F32)
        for number, piece in enumerate(pieces):
            disc_ref[date, number] = piece
        for piece in reversed(pieces):
            total = total + dot(ones, piece, NT)
        sums.append(total[0:1])
    sums = jnp.concatenate(sums, axis=0)
    a_src[...] = jnp.concatenate([sums[:, : K // 2], sums[:, K // 2 :]], axis=0)

    pl.semaphore_wait(barrier, MP + SC - 2)
    sends = to_scen(a_src, a_buf.at[sc], a_send, a_recv)
    for copy in sends:
        copy.start()
    a_buf[sc] = a_src[...]

    load.wait()
    picks = iota((32, K), 0)
    wanted = jnp.where(picks < KD, sc * KD + picks, picks - KD)
    chosen = ((iota((32, K), 1) == wanted) & (picks < KD + MONTHS)).astype(BF16)
    bond_labels = group_at(iota((PG, TILE), 0))

    def prepare(tile, income):
        at = pl.ds(pl.multiple_of(tile * TILE, TILE), TILE)
        pieces = parts(flows_ref[at, :], 3)
        for number, piece in enumerate(pieces):
            flow_parts[number, at, :] = piece
        found = dot(chosen, pieces[2], NT) + dot(chosen, pieces[1], NT) + dot(chosen, pieces[0], NT)
        chosen_ref[:, at] = found[:KD]
        groups = (bond_labels == block_ref[:, at]).astype(BF16)
        bond_ref[:, at] = groups
        return income + dot(stack_parts(found[KD : KD + 8], 3, 32), groups, NT)

    income = lax.fori_loop(0, B // TILE, prepare, jnp.zeros((32, PG), F32))
    income = income[0:8] + income[8:16] + income[16:24]

    point_labels = iota((PG, TILE), 0)
    accounts = jnp.zeros((32, PG), F32)
    for tile in range(M // TILE):
        at = pl.ds(tile * TILE, TILE)
        groups = (point_labels == group_ref[:, at]).astype(BF16)
        point_ref[:, at] = groups
        mass = jnp.where(iota((S, TILE), 0) == state_ref[:, at], account_ref[:, at], 0.0)
        accounts = accounts + dot(stack_parts(mass, 3, 32), groups, NT)
    accounts = accounts[0:8] + accounts[8:16] + accounts[16:24]

    move = []
    for s in range(S):
        row = transition_ref[s] + jnp.where(iota((S, PG), 0) == s, STAY_WEIGHT, 0.0)
        move.append(row / jnp.sum(row, axis=0, keepdims=True))
    powers = [move]
    for _ in range(MONTHS - 1):
        last = powers[-1]
        powers.append([functools.reduce(jnp.add, [last[s][v : v + 1] * move[v] for v in range(S)]) for s in range(S)])
    benefit = jnp.zeros((S, PG), F32)
    for u in range(S):
        benefit = jnp.where(iota((S, PG), 0) == u, benefit_ref[u], benefit)
    stays = [jnp.concatenate([power[s][0:1] for s in range(S)], axis=0) for power in powers]
    pays = [
        jnp.concatenate([jnp.sum(power[s] * benefit, axis=0, keepdims=True) for s in range(S)], axis=0)
        for power in powers
    ]

    def by_state(rows):
        return jnp.sum(accounts * rows, axis=0, keepdims=True)

    early = [accounts[0:1], by_state(stays[0]), by_state(stays[1]), by_state(pays[0]), by_state(pays[1]), by_state(pays[2])]
    early = swap_blocks(jnp.concatenate(early + [jnp.zeros((2, PG), F32)], axis=0))
    for q in range(MP // 2):
        e_src[q] = jnp.concatenate(
            [early[:, q * GQ : (q + 1) * GQ], income[:, q * GQ : (q + 1) * GQ], jnp.zeros((8, C - 2 * GQ), F32)], axis=1
        )
    e_copies = to_mp(lambda peer: e_src.at[pair(peer)], e_buf.at[mp], e_send, e_recv, mp_peers, mp)
    for copy in e_copies:
        copy.start()
    sends += e_copies
    e_buf[mp] = e_src[own]

    from_scen(a_src, lambda peer: a_buf.at[peer], a_send, a_recv)
    mean = a_buf[0]
    for slot in range(1, SC):
        mean = mean + a_buf[slot]
    mean = mean * (1.0 / SCEN)
    mean = stack_parts(jnp.concatenate([mean[0:4], mean[4:8]], axis=1), 3, 16)

    def weigh(tile, total):
        at = pl.ds(pl.multiple_of(tile * TILE, TILE), TILE)
        high = dot(mean, flow_parts[0, at, :], NT)
        middle = dot(mean, flow_parts[1, at, :], NT)
        low = dot(mean, flow_parts[2, at, :], NT)
        price = high[0:4] + ((high[4:8] + middle[0:4]) + (high[8:12] + middle[4:8] + low[0:4]))
        weight = target_ref[:, at] / price
        flows = chosen_ref[:, at]
        scaled = jnp.concatenate([weight[date : date + 1] * flows for date in range(DATES)], axis=0)
        return total + dot(stack_parts(scaled, 3, 3 * DATES * KD), bond_ref[:, at], NT)

    worth = lax.fori_loop(0, B // TILE, weigh, jnp.zeros((3 * DATES * KD, PG), F32))
    size = DATES * KD
    worth = worth[0:size] + (worth[size : 2 * size] + worth[2 * size :])
    for q in range(MP // 2):
        b_src[q] = jnp.concatenate(
            [worth[date * KD : (date + 1) * KD, q * GQ : (q + 1) * GQ] for date in range(DATES)], axis=1
        )
    b_copies = to_mp(lambda peer: b_src.at[pair(peer)], b_buf.at[mp], b_send, b_recv, mp_peers, mp)
    for copy in b_copies:
        copy.start()
    sends += b_copies
    b_buf[mp] = b_src[own]

    local = [rows_ref[0:3], stays[0][0:1], stays[1][0:1], pays[0][0:1], pays[1][0:1], pays[2][0:1]]
    local = jnp.concatenate(local, axis=0)
    order = (group_at(iota((PG, PG), 0)) == iota((PG, PG), 1)).astype(F32)
    cols_ref[...] = dot(order, local, NT, EXACT)
    first_ref[...] = dot(order, start_ref[...], NT, EXACT)
    twice = jnp.broadcast_to(cols_ref[:, 2:3] * 2.0, (PG, C))
    pre_ref[0] = twice
    pre_ref[1] = twice * jax.nn.sigmoid(LAPSE_SLOPE * (rates[0:1] - first_ref[...]))
    pre_ref[2] = first_ref[...]

    gathered = jnp.concatenate(powers[2] + [powers[1][0], powers[0][0], stays[1], stays[0]], axis=0)
    gathered = stack_parts(gathered, 2, 192)
    for tile in range(M // TILE):
        at = pl.ds(tile * TILE, TILE)
        found = dot(gathered, point_ref[:, at], NN)
        found = found[0:96] + found[96:192]
        states = state_ref[:, at]
        last = jnp.zeros((S, TILE), F32)
        for s in range(S):
            last = jnp.where(states == s, found[s * S : (s + 1) * S], last)
        held = iota((S, TILE), 0) == states
        second = jnp.sum(jnp.where(held, found[80:88], 0.0), axis=0, keepdims=True)
        first = jnp.sum(jnp.where(held, found[88:96], 0.0), axis=0, keepdims=True)
        start = (states == 0).astype(F32)
        table_ref[0:8, at] = last
        table_ref[8:16, at] = found[0:8]
        table_ref[16:24, at] = found[64:72]
        table_ref[24:32, at] = found[72:80]
        table_ref[32:40, at] = jnp.concatenate(
            [start, first, second, account_ref[:, at], jnp.zeros((4, TILE), F32)], axis=0
        )

    from_mp(lambda peer: b_src.at[pair(peer)], lambda peer: b_buf.at[peer], b_send, b_recv, mp_peers, lambda peer: peer)
    total = b_buf[0]
    for slot in range(1, MP):
        total = total + b_buf[slot]
    rows = pl.ds(pl.multiple_of(sc * KD, KD), KD)
    c_buf[rows, :] = total
    copies = to_scen(c_buf.at[rows, :], c_buf.at[rows, :], c_send, c_recv)
    for copy in copies:
        copy.start()
    sends += copies

    from_mp(lambda peer: e_src.at[pair(peer)], lambda peer: e_buf.at[peer], e_send, e_recv, mp_peers, lambda peer: peer)
    early = e_buf[0]
    for slot in range(1, MP):
        early = early + e_buf[slot]
    early = jnp.transpose(jnp.concatenate([early, jnp.zeros((C - 8, C), F32)], axis=0))
    income = early[GQ : 2 * GQ]
    mine = pl.ds(pl.multiple_of(own * GQ, GQ), GQ)
    columns = cols_ref[mine, :]
    guarantee, spread, lapse_base = columns[:, 0:1], columns[:, 1:2], columns[:, 2:3]
    stay = [columns[:, 3:4], columns[:, 4:5]]
    pay = [columns[:, 5:6], columns[:, 6:7], columns[:, 7:8]]
    credited = first_ref[mine, :]

    def rows_at(peer):
        return pl.ds(pl.multiple_of(peer * KD, KD), KD)

    from_scen(c_buf.at[rows, :], lambda peer: c_buf.at[rows_at(peer), :], c_send, c_recv)
    worth = jnp.transpose(c_buf[...])
    assets = []
    for date in range(DATES):
        pieces = stack_parts(worth[date * GQ : (date + 1) * GQ], 3, 3 * GQ)
        high = dot(pieces, disc_ref[date, 0], NN)
        middle = dot(pieces[: 2 * GQ], disc_ref[date, 1], NN)
        low = dot(pieces[:GQ], disc_ref[date, 2], NN)
        assets.append(
            high[:GQ] + ((high[GQ : 2 * GQ] + middle[:GQ]) + (high[2 * GQ :] + middle[GQ:] + low))
        )

    growth = jnp.ones((GQ, C), F32)
    present = jnp.zeros((GQ, C), F32)
    lapses = []
    for month in range(MONTHS):
        factor = lapse_base * 2.0 * jax.nn.sigmoid(LAPSE_SLOPE * (rates[month : month + 1] - credited))
        mass = early[:GQ, month : month + 1]
        for lag, lapse in enumerate(reversed(lapses)):
            mass = mass - lapse * stay[lag]
        lapses.append(mass * factor)
        growth = growth * (1.0 + credited / 12.0)
        paid = early[:GQ, 3 + month : 4 + month]
        for lag, lapse in enumerate(reversed(lapses)):
            paid = paid - lapse * pay[lag]
        flows = growth * (lapses[-1] + paid)
        held = assets[month]
        later = assets[month + 1] + income[:, month : month + 1]
        earned = 12.0 * (later - held) / held
        credited = jnp.maximum(
            guarantee, 0.5 * credited + 0.5 * (earned - spread) - LIQUID_CHARGE * flows / held
        )
        if month < MONTHS - 1:
            d_buf[mine, month * C : (month + 1) * C] = credited
        present = present + flows * jnp.exp(-rates[month + 1 : month + 2] * ((month + 1) / 12.0))
    d_copies = to_mp(lambda peer: d_buf.at[mine, :], d_buf.at[mine, :], d_send, d_recv, near_peers, own)
    for copy in d_copies:
        copy.start()
    half = jnp.where(zh == 0, present[:16], present[16:])
    f_src[...] = dot(jnp.ones((8, C), F32), jnp.concatenate([half, jnp.zeros((C - 16, C), F32)], axis=0), NT, EXACT)
    f_copies = to_scen(f_src, f_buf.at[sc], f_send, f_recv)
    for copy in f_copies:
        copy.start()
    sends += d_copies + f_copies
    f_buf[sc] = f_src[...]
    credited_ref[...] = 100.0 * jnp.where(zh == 0, credited[:16], credited[16:])

    def pair_rows(peer):
        return pl.ds(pl.multiple_of(pair(peer) * GQ, GQ), GQ)

    from_mp(lambda peer: d_buf.at[mine, :], lambda peer: d_buf.at[pair_rows(peer), :], d_send, d_recv, near_peers, pair)
    rho_ref[...] = d_buf[...]
    from_scen(f_src, lambda peer: f_buf.at[peer], f_send, f_recv)
    value = f_buf[0]
    for slot in range(1, SC):
        value = value + f_buf[slot]
    value_ref[...] = value * (1.0 / SCEN)
    for copy in sends:
        copy.wait_send()


CHUNK = 32


def output_kernel(
    group_ref, path_ref, rho_ref, pre_ref, table_ref, credited_in, value_in,
    occupancy_hbm, account_hbm, credited_ref, value_ref,
    point_ref, occupancy_ref, account_ref, sems,
):
    credited_ref[...] = credited_in[...]
    value_ref[...] = value_in[0:1, 0:16]
    labels = group_at(iota((PG, TILE), 0))
    for tile in range(M // TILE):
        at = pl.ds(tile * TILE, TILE)
        point_ref[:, at] = (labels == group_ref[:, at]).astype(BF16)
    twice = pre_ref[0]
    rho = [pre_ref[2], rho_ref[:, :C], rho_ref[:, C:]]
    tables = [pre_ref[1]]
    for month in (1, 2):
        tables.append(twice * jax.nn.sigmoid(LAPSE_SLOPE * (path_ref[month : month + 1, :] - rho[month])))
    grown = [rate / 12.0 for rate in rho]
    gain = grown[0] + grown[1] + grown[0] * grown[1]
    tables.append(gain + grown[2] + gain * grown[2])
    tables = [parts(jnp.transpose(table), 2) for table in tables]

    copies = []
    for chunk in range(C // CHUNK):
        rows = slice(chunk * CHUNK, (chunk + 1) * CHUNK)
        lhs = jnp.concatenate([piece[rows] for table in tables for piece in table], axis=0)
        for tile in range(M // TILE):
            at = pl.ds(tile * TILE, TILE)
            found = dot(lhs, point_ref[:, at], NN)
            found = [
                found[2 * n * CHUNK : (2 * n + 1) * CHUNK] + found[(2 * n + 1) * CHUNK : (2 * n + 2) * CHUNK]
                for n in range(4)
            ]
            first = found[0] * table_ref[32:33, at]
            second = (table_ref[33:34, at] - first * table_ref[24:25, at]) * found[1]
            third = (table_ref[34:35, at] - first * table_ref[16:17, at] - second * table_ref[24:25, at]) * found[2]
            for u in range(S):
                occupancy_ref[u, rows, at] = (
                    table_ref[u : u + 1, at]
                    - first * table_ref[8 + u : 9 + u, at]
                    - second * table_ref[16 + u : 17 + u, at]
                    - third * table_ref[24 + u : 25 + u, at]
                )
            account = table_ref[35:36, at]
            account_ref[rows, at] = account + account * found[3]
        copies.append(pltpu.make_async_copy(occupancy_ref.at[:, rows, :], occupancy_hbm.at[:, rows, :], sems.at[0, chunk]))
        copies.append(pltpu.make_async_copy(account_ref.at[rows, :], account_hbm.at[rows, :], sems.at[1, chunk]))
        copies[-2].start()
        copies[-1].start()
    for copy in copies:
        copy.wait()


def vmem(*shape):
    return pltpu.VMEM(shape, F32)


def body(
    group_id,
    issue_state,
    account_start,
    transition,
    lapse_base,
    benefit,
    bond_block,
    bond_flows,
    bond_target,
    base_rate,
    rate_moves,
    guarantee,
    spread,
    start_rate,
):
    in_vmem = pl.BlockSpec(memory_space=pltpu.VMEM)
    in_smem = pl.BlockSpec(memory_space=pltpu.SMEM)
    anywhere = pl.BlockSpec(memory_space=pl.ANY)
    groups = group_id.reshape(1, M)
    dma = pltpu.SemaphoreType.DMA
    rho, pre, table, credited, value, path = pl.pallas_call(
        exchange_kernel,
        out_shape=[
            jax.ShapeDtypeStruct((PG, 2 * C), F32),
            jax.ShapeDtypeStruct((3, PG, C), F32),
            jax.ShapeDtypeStruct((40, M), F32),
            jax.ShapeDtypeStruct((16, C), F32),
            jax.ShapeDtypeStruct((8, C), F32),
            jax.ShapeDtypeStruct((8, C), F32),
        ],
        in_specs=[in_vmem] * 5 + [in_smem, in_vmem, anywhere] + [in_vmem] * 4,
        out_specs=[in_vmem] * 6,
        scratch_shapes=[
            vmem(B, K),
            pltpu.VMEM((3, B, K), BF16),
            vmem(KD, B),
            pltpu.VMEM((PG, B), BF16),
            pltpu.VMEM((PG, M), BF16),
            pltpu.VMEM((DATES, 3, K, C), BF16),
            vmem(PG, 8),
            vmem(PG, C),
            vmem(8, C),
            vmem(SC, 8, C),
            vmem(MP // 2, 8, C),
            vmem(MP, 8, C),
            vmem(MP // 2, KD, C),
            vmem(MP, KD, C),
            vmem(K, C),
            vmem(PG, 2 * C),
            vmem(8, C),
            vmem(SC, 8, C),
            dma,
            dma((SC,)), dma((SC,)),
            dma((MP,)), dma((MP,)),
            dma((MP,)), dma((MP,)),
            dma((SC,)), dma((SC,)),
            dma((MP,)), dma((MP,)),
            dma((SC,)), dma((SC,)),
        ],
        compiler_params=pltpu.CompilerParams(
            collective_id=0, has_side_effects=True, vmem_limit_bytes=VMEM_LIMIT
        ),
        name="exchange",
    )(
        groups,
        issue_state.reshape(1, M),
        account_start.reshape(1, M),
        transition.transpose(1, 2, 0),
        jnp.stack([guarantee, spread, lapse_base]),
        benefit,
        bond_block.reshape(1, B),
        bond_flows,
        bond_target.reshape(1, B),
        base_rate.reshape(1, C),
        rate_moves,
        start_rate,
    )
    occupancy, account_value, credited, value = pl.pallas_call(
        output_kernel,
        out_shape=[
            jax.ShapeDtypeStruct((S, C, M), F32),
            jax.ShapeDtypeStruct((C, M), F32),
            jax.ShapeDtypeStruct((16, C), F32),
            jax.ShapeDtypeStruct((1, 16), F32),
        ],
        in_specs=[in_vmem] * 7,
        out_specs=[anywhere, anywhere, in_vmem, in_vmem],
        scratch_shapes=[pltpu.VMEM((PG, M), BF16), vmem(S, C, M), vmem(C, M), dma((2, C // CHUNK))],
        compiler_params=pltpu.CompilerParams(vmem_limit_bytes=VMEM_LIMIT),
        name="outputs",
    )(groups, path, rho, pre, table, credited, value)
    return occupancy, account_value, credited.T, value.reshape(16)


def solution(mesh):
    placed = (
        P("mp"),
        P("mp"),
        P("mp"),
        P(),
        P(),
        P(),
        P("mp", None),
        P("mp", None),
        P("mp"),
        P("scen"),
        P(None, "scen"),
        P(),
        P(),
        P("scen", None),
    )
    return jax.shard_map(
        body,
        mesh=mesh,
        in_specs=placed,
        out_specs=(P(None, "scen", "mp"), P("scen", "mp"), P("scen", "mp"), P("mp")),
        check_vma=False,
    )
```

time: 773 us -> 53.8 us (0.07)
  the two profiles are of different devices: /device:TPU:0 before, /device:TPU:1 now
where the time goes in v2:
time: 53.8 us; the launch traced here: 53.4 us
  Pallas kernels  43 us (80%)
  local copies, waits for them, and re-layouts  8.94 us (17%)
  other arithmetic  0.72 us (1%)
  between operations  0.65 us (1%)
    pallas_call x1, Pallas kernels, body(): pl.pallas_call(exchange_kernel, out_shape=[jax.ShapeDtypeStruct((PG, 2 *...  39.4 us
    unnamed x20, local copies, waits for them, and re-layouts  8.23 us
    pallas_call x1, Pallas kernels, body(): pl.pallas_call(output_kernel, out_shape=[jax.ShapeDtypeStruct((S, C, M),...  3.6 us

profile of v2, /device:TPU:1, one launch (start us, length us, event | category | flops | bytes accessed | tf_op | source)
XLA Modules:
  0.0 53.4 jit_solution(7264764492745889631)
XLA Ops:
  0.6 0.7 %pad_maximum_fusion.rows_ref = f32[3,256]{1,0:T(4,128)S(1)} fusion(f32[1,256]{1,0:T(1,128)} %bitcast.18, f32[1,256]{1,0:T(1,128)} %bitcast.19, f32[1,256]{1,0:T(1,128)} %bitcast.20), kind=kLoop, calls=%fused_computation | loop fusion | flops 1536 | bytes 6144 | tf_op jit(solution)/shard_map/stack | solution.py:557
  1.4 0.7 %reshape.33.target_ref = f32[1,2560]{1,0:T(1,128)S(1)} reshape(f32[2560]{0:T(1024)} %param.22) | data formatting | bytes 20480 | tf_op jit(solution)/shard_map/reshape | solution.py:561
  2.1 0.0 copy-start
  2.1 1.7 %copy-done = f32[2560,256]{1,0:T(8,128)S(1)} copy-done((f32[2560,256]{1,0:T(8,128)S(1)}, f32[2560,256]{1,0:T(8,128)}, u32[]{:S(2)}) %copy-start) | copy-done | bytes 2621464
  3.8 0.0 copy-start.1
  3.8 0.9 %copy-done.1 = f32[128,256]{1,0:T(8,128)S(1)} copy-done((f32[128,256]{1,0:T(8,128)S(1)}, f32[128,256]{1,0:T(8,128)}, u32[]{:S(2)}) %copy-start.1) | copy-done | bytes 131096
  4.7 0.0 copy-start.2
  4.7 0.8 %copy-done.2 = f32[256,8,8]{0,2,1:T(8,128)S(1)} copy-done((f32[256,8,8]{0,2,1:T(8,128)S(1)}, f32[256,8,8]{0,2,1:T(8,128)}, u32[]{:S(2)}) %copy-start.2) | copy-done | bytes 65560
  5.6 0.0 copy-start.3
  5.6 0.7 %copy-done.3 = s32[1024]{0:T(1024)S(1)} copy-done((s32[1024]{0:T(1024)S(1)}, s32[1024]{0:T(1024)}, u32[]{:S(2)}) %copy-start.3) | copy-done | bytes 4120
  6.2 0.0 copy-start.4
  6.2 0.7 %copy-done.4 = s32[2560,1]{0,1:T(1,128)S(1)} copy-done((s32[2560,1]{0,1:T(1,128)S(1)}, s32[2560,1]{0,1:T(1,128)}, u32[]{:S(2)}) %copy-start.4) | copy-done | bytes 10264
  6.9 0.0 copy-start.5
  6.9 0.7 %copy-done.5 = s32[1024]{0:T(1024)S(1)} copy-done((s32[1024]{0:T(1024)S(1)}, s32[1024]{0:T(1024)}, u32[]{:S(2)}) %copy-start.5) | copy-done | bytes 4120
  7.6 0.0 copy-start.6
  7.6 0.7 %copy-done.6 = f32[1024]{0:T(1024)S(1)} copy-done((f32[1024]{0:T(1024)S(1)}, f32[1024]{0:T(1024)}, u32[]{:S(2)}) %copy-start.6) | copy-done | bytes 4120
  8.3 0.0 copy-start.7
  8.3 0.7 %copy-done.7 = f32[3,128]{1,0:T(4,128)S(1)} copy-done((f32[3,128]{1,0:T(4,128)S(1)}, f32[3,128]{1,0:T(4,128)}, u32[]{:S(2)}) %copy-start.7) | copy-done | bytes 1560
  9.0 0.0 copy-start.8
  9.0 0.7 %copy-done.8 = f32[8]{0:T(128)S(1)} copy-done((f32[8]{0:T(128)S(1)}, f32[8]{0:T(128)}, u32[]{:S(2)}) %copy-start.8) | copy-done | bytes 56
  9.7 0.0 copy-start.9
  9.7 0.7 %copy-done.9 = f32[128]{0:T(128)S(1)} copy-done((f32[128]{0:T(128)S(1)}, f32[128]{0:T(128)}, u32[]{:S(2)}) %copy-start.9) | copy-done | bytes 536
  10.3 39.4 %exchange.1 = (f32[256,256]{1,0:T(8,128)S(1)}, f32[3,256,128]{2,1,0:T(8,128)S(1)}, f32[40,1024]{1,0:T(8,128)S(1)}, f32[16,128]{1,0:T(8,128)S(1)}, f32[8,128]{1,0:T(8,128)S(1)}, /*index=5*/f32[8,128]{1,0:T(8,128)S(1)}) custom-call(s32[1,1024]{1,0:T(1,128)S(1)} %bitcast.12, s32[1,1024]{1,0:T(1,128)S(1)} %bitcast.15, f32[1,1024]{1,0:T(1,128)S(1)} %bitcast.16, ...), custom_call_target="tpu_custom_call" | custom-call | tf_op jit(solution)/shard_map/exchange/pallas_call | solution.py:509
  49.8 3.6 %outputs.1 = (f32[8,128,1024]{2,1,0:T(8,128)}, f32[128,1024]{1,0:T(8,128)}, f32[16,128]{1,0:T(8,128)}, f32[1,16]{1,0:T(1,128)}) custom-call(s32[1,1024]{1,0:T(1,128)S(1)} %bitcast.13, f32[8,128]{1,0:T(8,128)S(1)} %get-tuple-element.14.path_ref, f32[256,256]{1,0:T(8,128)S(1)} %get-tuple-element.15.rho_ref, f32[3,256,128]{2,1,0:T(8,128)S(1)} %get-tuple-element.16.pre_ref, ...), custom_call_target="tpu_custom_call" | custom-call | tf_op jit(solution)/shard_map/outputs/pallas_call | solution.py:566
Async XLA Ops:
  2.1 1.7 %copy-start = (f32[2560,256]{1,0:T(8,128)S(1)}, f32[2560,256]{1,0:T(8,128)}, u32[]{:S(2)}) copy-start(f32[2560,256]{1,0:T(8,128)} %flows_hbm.1) | copy-start | bytes 7864324
  3.8 0.9 %copy-start.1 = (f32[128,256]{1,0:T(8,128)S(1)}, f32[128,256]{1,0:T(8,128)}, u32[]{:S(2)}) copy-start(f32[128,256]{1,0:T(8,128)} %start_ref.1) | copy-start | bytes 393220
  4.7 0.8 %copy-start.2 = (f32[256,8,8]{0,2,1:T(8,128)S(1)}, f32[256,8,8]{0,2,1:T(8,128)}, u32[]{:S(2)}) copy-start(f32[256,8,8]{0,2,1:T(8,128)} %param.17) | copy-start | bytes 196612
  5.6 0.7 %copy-start.3 = (s32[1024]{0:T(1024)S(1)}, s32[1024]{0:T(1024)}, u32[]{:S(2)}) copy-start(s32[1024]{0:T(1024)} %param.14) | copy-start | bytes 12292
  6.2 0.7 %copy-start.4 = (s32[2560,1]{0,1:T(1,128)S(1)}, s32[2560,1]{0,1:T(1,128)}, u32[]{:S(2)}) copy-start(s32[2560,1]{0,1:T(1,128)} %param.20) | copy-start | bytes 30724
  6.9 0.7 %copy-start.5 = (s32[1024]{0:T(1024)S(1)}, s32[1024]{0:T(1024)}, u32[]{:S(2)}) copy-start(s32[1024]{0:T(1024)} %param.15) | copy-start | bytes 12292
  7.6 0.7 %copy-start.6 = (f32[1024]{0:T(1024)S(1)}, f32[1024]{0:T(1024)}, u32[]{:S(2)}) copy-start(f32[1024]{0:T(1024)} %param.16) | copy-start | bytes 12292
  8.3 0.7 %copy-start.7 = (f32[3,128]{1,0:T(4,128)S(1)}, f32[3,128]{1,0:T(4,128)}, u32[]{:S(2)}) copy-start(f32[3,128]{1,0:T(4,128)} %moves_ref.1) | copy-start | bytes 4612
  9.0 0.7 %copy-start.8 = (f32[8]{0:T(128)S(1)}, f32[8]{0:T(128)}, u32[]{:S(2)}) copy-start(f32[8]{0:T(128)} %benefit_ref.1) | copy-start | bytes 100
  9.7 0.7 %copy-start.9 = (f32[128]{0:T(128)S(1)}, f32[128]{0:T(128)}, u32[]{:S(2)}) copy-start(f32[128]{0:T(128)} %param.23) | copy-start | bytes 1540

commit v3 on v2

v3 whole, which is shorter than its diff:
```python
import functools

import jax
import jax.numpy as jnp
from jax import lax
from jax.experimental import pallas as pl
from jax.experimental.pallas import tpu as pltpu
from jax.sharding import PartitionSpec as P

MESH = pl.DeviceIdType.MESH
EXACT = lax.Precision.HIGHEST
F32, BF16 = jnp.float32, jnp.bfloat16
STAY_WEIGHT = 40.0
LAPSE_SLOPE = 30.0
LIQUID_CHARGE = 0.5

S = 8
PG = 256
K = 256
DATES = 4
MONTHS = 3
C = 128
M = 1024
B = 2560
TILE = 256
MP = 16
SC = 16
SCEN = C * SC
KD = K // SC
GQ = 2 * PG // MP
VMEM_LIMIT = 56 * 1024 * 1024

NT = (((1,), (1,)), ((), ()))
NN = (((1,), (0,)), ((), ()))


def dot(a, b, dims, precision=None):
    return lax.dot_general(a, b, dims, precision=precision, preferred_element_type=F32)


def parts(x, count):
    found = []
    for _ in range(count):
        found.append(x.astype(BF16))
        x = x - found[-1].astype(F32)
    return found


def stack_parts(x, count, rows):
    found = parts(x, count)
    pieces = [piece.astype(F32) for piece in found]
    rest = rows - count * x.shape[0]
    if rest:
        pieces.append(jnp.zeros((rest, x.shape[1]), F32))
    return jnp.concatenate(pieces, axis=0).astype(BF16)


def iota(shape, axis):
    return lax.broadcasted_iota(jnp.int32, shape, axis)


def group_at(place):
    block = place // 16
    return (block // 4 * 4 + block % 2 * 2 + block // 2 % 2) * 16 + place % 16


def swap_blocks(rows):
    block = iota(rows.shape, 1) // 16 % 4
    width = rows.shape[1]
    up = pltpu.roll(rows, width - 16, 1)
    down = pltpu.roll(rows, 16, 1)
    return jnp.where(block == 1, up, jnp.where(block == 2, down, rows))


def discounts(rates, date):
    horizon = iota((K, C), 0)
    tenor = (horizon - date + 1).astype(F32) / 12.0
    factor = jnp.exp(-tenor * rates[date : date + 1, :])
    return jnp.where(horizon >= date, factor, 0.0) if date else factor


def exchange_kernel(
    base_hbm,
    moves_hbm,
    block_hbm,
    flows_hbm,
    group_hbm,
    state_hbm,
    account_hbm,
    transition_hbm,
    benefit_hbm,
    guarantee_hbm,
    spread_hbm,
    lapse_hbm,
    target_hbm,
    start_hbm,
    rho_hbm,
    pre_hbm,
    table_hbm,
    lapse1_hbm,
    point_hbm,
    small_hbm,
    value_hbm,
    pre_ref,
    table_ref,
    lapse1_ref,
    point_ref,
    small_ref,
    base_ref,
    moves_ref,
    block_ref,
    flows_ref,
    group_ref,
    state_ref,
    account_ref,
    transition_ref,
    benefit_ref,
    guarantee_ref,
    spread_ref,
    lapse_ref,
    target_ref,
    start_ref,
    flow_parts,
    chosen_ref,
    bond_ref,
    disc_ref,
    cols_ref,
    first_ref,
    a_src,
    a_buf,
    e_src,
    e_buf,
    b_src,
    b_buf,
    c_buf,
    d_src,
    f_src,
    load_sem,
    store_sem,
    a_send,
    a_recv,
    e_send,
    e_recv,
    b_send,
    b_recv,
    c_send,
    c_recv,
    d_send,
    d_recv,
    f_send,
    f_recv,
):
    mp, sc = lax.axis_index("mp"), lax.axis_index("scen")
    x, zh, core = mp // 4, mp // 2 % 2, mp % 2
    own = x * 2 + core
    zl, y = sc // 4, sc % 4

    def mp_index(dx, dz, dc):
        return (x + dx) % 4 * 4 + (zh + dz) % 2 * 2 + (core + dc) % 2

    def months_of(scen, half):
        return (scen // 4 + 2 * half) % 4 * 4 + scen % 4

    def scen_peer(dz, dy):
        there = (zl + dz) % 4
        across = (there - zl) * (there - zl) // 9
        return mp_index(0, across, 0), there * 4 + (y + dy) % 4

    steps = [(dz, dy) for dz in (2, 1, 3, 0) for dy in (2, 1, 3, 0) if (dz, dy) != (0, 0)]
    a_peers = [scen_peer(dz, dy) for dz, dy in steps]
    c_peers = [(mp, (zl + dz) % 4 * 4 + (y + dy) % 4) for dz, dy in steps]
    b_peers = [
        (mp_index(dx, dz, dc), (zl + 2 * dz) % 4 * 4 + y)
        for dz in (1, 0)
        for dx in (2, 1, 3, 0)
        for dc in (0, 1)
        if (dx, dz, dc) != (0, 0, 0)
    ]
    d_peers = [(mp_index(dx, 0, dc), sc) for dx in (2, 1, 3, 0) for dc in (0, 1) if (dx, dc) != (0, 0)]

    barrier = pltpu.get_barrier_semaphore()
    for peer in a_peers + b_peers + c_peers:
        pl.semaphore_signal(barrier, inc=1, device_id=peer, device_id_type=MESH)
    loads = [
        pltpu.make_async_copy(src, dst, load_sem.at[n])
        for n, (src, dst) in enumerate(
            [
                (base_hbm, base_ref),
                (moves_hbm, moves_ref),
                (block_hbm, block_ref),
                (flows_hbm, flows_ref),
                (group_hbm, group_ref),
                (state_hbm, state_ref),
                (account_hbm, account_ref),
                (transition_hbm, transition_ref),
                (benefit_hbm, benefit_ref),
                (guarantee_hbm, guarantee_ref),
                (spread_hbm, spread_ref),
                (lapse_hbm, lapse_ref),
                (target_hbm, target_ref),
                (start_hbm, start_ref),
            ]
        )
    ]
    for load in loads:
        load.start()

    def send_to(peers, src, dst, sems, mark):
        copies = [
            pltpu.make_async_remote_copy(
                src_ref=src(peer), dst_ref=dst, send_sem=sems[0].at[n], recv_sem=sems[1].at[mark],
                device_id=peer, device_id_type=MESH,
            )
            for n, peer in enumerate(peers)
        ]
        for copy in copies:
            copy.start()
        return copies

    def wait_from(peers, src, slot, sems, mark):
        for n, peer in enumerate(peers):
            pltpu.make_async_remote_copy(
                src_ref=src(peer), dst_ref=slot(peer), send_sem=sems[0].at[n], recv_sem=sems[1].at[mark(peer)],
                device_id=peer, device_id_type=MESH,
            ).wait_recv()

    def pair(peer):
        return peer[0] // 4 * 2 + peer[0] % 2

    a_sems, b_sems, c_sems = (a_send, a_recv), (b_send, b_recv), (c_send, c_recv)
    d_sems, e_sems, f_sems = (d_send, d_recv), (e_send, e_recv), (f_send, f_recv)
    months = months_of(sc, zh)

    for load in loads[:2]:
        load.wait()
    rates = [base_ref[...]]
    for month in range(MONTHS):
        rates.append(rates[-1] + moves_ref[month : month + 1, :])
    rates = jnp.concatenate(rates, axis=0)
    blank = jnp.zeros((8, C), F32)
    small_ref[16:32, :] = jnp.concatenate([blank, rates, blank[:4]], axis=0)
    ones = jnp.ones((16, C), BF16)
    sums = []
    for date in range(DATES):
        pieces = parts(discounts(rates, date), 3)
        total = jnp.zeros((16, K), F32)
        for number, piece in enumerate(pieces):
            disc_ref[date, number] = piece
        for piece in reversed(pieces):
            total = total + dot(ones, piece, NT)
        sums.append(total[0:1])
    sums = jnp.concatenate(sums, axis=0)
    a_src[...] = jnp.concatenate([sums[:, : K // 2], sums[:, K // 2 :]], axis=0)

    pl.semaphore_wait(barrier, len(a_peers + b_peers + c_peers))
    sends = send_to(a_peers, lambda peer: a_src, a_buf.at[sc], a_sems, sc)
    a_buf[sc] = a_src[...]

    for load in loads[2:4]:
        load.wait()
    picks = iota((32, K), 0)
    wanted = jnp.where(picks < KD, months * KD + picks, picks - KD)
    chosen = ((iota((32, K), 1) == wanted) & (picks < KD + MONTHS)).astype(BF16)
    bond_labels = group_at(iota((PG, TILE), 0))

    def prepare(tile, income):
        at = pl.ds(pl.multiple_of(tile * TILE, TILE), TILE)
        pieces = parts(flows_ref[at, :], 3)
        for number, piece in enumerate(pieces):
            flow_parts[number, at, :] = piece
        found = dot(chosen, pieces[2], NT) + dot(chosen, pieces[1], NT) + dot(chosen, pieces[0], NT)
        chosen_ref[:, at] = found[:KD]
        groups = (bond_labels == block_ref[:, at]).astype(BF16)
        bond_ref[:, at] = groups
        return income + dot(stack_parts(found[KD : KD + 8], 3, 32), groups, NT)

    income = lax.fori_loop(0, B // TILE, prepare, jnp.zeros((32, PG), F32))
    income = income[0:8] + income[8:16] + income[16:24]

    for load in loads[4:]:
        load.wait()
    accounts = jnp.zeros((32, PG), F32)
    for tile in range(M // TILE):
        at = pl.ds(tile * TILE, TILE)
        groups = (bond_labels == group_ref[:, at]).astype(BF16)
        point_ref[:, at] = groups
        mass = jnp.where(iota((S, TILE), 0) == state_ref[:, at], account_ref[:, at], 0.0)
        accounts = accounts + dot(stack_parts(mass, 3, 32), groups, NT)
    accounts = accounts[0:8] + accounts[8:16] + accounts[16:24]

    move = []
    for s in range(S):
        row = transition_ref[s] + jnp.where(iota((S, PG), 0) == s, STAY_WEIGHT, 0.0)
        move.append(row / jnp.sum(row, axis=0, keepdims=True))
    powers = [move]
    for _ in range(MONTHS - 1):
        last = powers[-1]
        powers.append([functools.reduce(jnp.add, [last[s][v : v + 1] * move[v] for v in range(S)]) for s in range(S)])
    benefit = jnp.where(iota((S, S), 0) == iota((S, S), 1), benefit_ref[...], 0.0)
    benefit = jnp.sum(benefit, axis=1, keepdims=True)
    stays = [jnp.concatenate([power[s][0:1] for s in range(S)], axis=0) for power in powers]
    pays = [
        jnp.concatenate([jnp.sum(power[s] * benefit, axis=0, keepdims=True) for s in range(S)], axis=0)
        for power in powers
    ]

    def by_state(rows):
        return jnp.sum(accounts * swap_blocks(rows), axis=0, keepdims=True)

    early = [accounts[0:1], by_state(stays[0]), by_state(stays[1]), by_state(pays[0]), by_state(pays[1]), by_state(pays[2])]
    early = jnp.concatenate(early + [jnp.zeros((2, PG), F32)], axis=0)
    for q in range(MP // 2):
        e_src[q] = jnp.concatenate(
            [early[:, q * GQ : (q + 1) * GQ], income[:, q * GQ : (q + 1) * GQ], jnp.zeros((8, C - 2 * GQ), F32)], axis=1
        )
    sends += send_to(b_peers, lambda peer: e_src.at[pair(peer)], e_buf.at[mp], e_sems, mp)
    e_buf[mp] = e_src[own]

    wait_from(a_peers, lambda peer: a_src, lambda peer: a_buf.at[peer[1]], a_sems, lambda peer: peer[1])
    mean = a_buf[0]
    for slot in range(1, SC):
        mean = mean + a_buf[slot]
    mean = mean * (1.0 / SCEN)
    mean = stack_parts(jnp.concatenate([mean[0:4], mean[4:8]], axis=1), 3, 16)

    def weigh(tile, total):
        at = pl.ds(pl.multiple_of(tile * TILE, TILE), TILE)
        high = dot(mean, flow_parts[0, at, :], NT)
        middle = dot(mean, flow_parts[1, at, :], NT)
        low = dot(mean, flow_parts[2, at, :], NT)
        price = high[0:4] + ((high[4:8] + middle[0:4]) + (high[8:12] + middle[4:8] + low[0:4]))
        target = [target_ref[pl.ds(tile * 2 + n, 1), :] for n in range(2)]
        weight = jnp.concatenate(target, axis=1) / price
        flows = chosen_ref[:, at]
        scaled = jnp.concatenate([weight[date : date + 1] * flows for date in range(DATES)], axis=0)
        return total + dot(stack_parts(scaled, 3, 3 * DATES * KD), bond_ref[:, at], NT)

    worth = lax.fori_loop(0, B // TILE, weigh, jnp.zeros((3 * DATES * KD, PG), F32), unroll=True)
    size = DATES * KD
    worth = worth[0:size] + (worth[size : 2 * size] + worth[2 * size :])
    for q in range(MP // 2):
        b_src[q] = jnp.concatenate(
            [worth[date * KD : (date + 1) * KD, q * GQ : (q + 1) * GQ] for date in range(DATES)], axis=1
        )
    sends += send_to(b_peers, lambda peer: b_src.at[pair(peer)], b_buf.at[mp], b_sems, mp)
    b_buf[mp] = b_src[own]

    local = [guarantee_ref[...], spread_ref[...], lapse_ref[...], stays[0][0:1], stays[1][0:1], pays[0][0:1], pays[1][0:1], pays[2][0:1]]
    local = jnp.concatenate(local, axis=0)
    order = (group_at(iota((PG, PG), 0)) == iota((PG, PG), 1)).astype(F32)
    cols_ref[...] = dot(order, local, NT, EXACT)
    first_ref[...] = dot(order, start_ref[...], NT, EXACT)
    twice = jnp.broadcast_to(cols_ref[:, 2:3] * 2.0, (PG, C))
    pre_ref[0] = twice
    pre_ref[1] = first_ref[...]
    start_lapse = twice * jax.nn.sigmoid(LAPSE_SLOPE * (rates[0:1] - first_ref[...]))
    start_lapse = stack_parts(jnp.transpose(start_lapse), 2, 2 * C)

    gathered = jnp.concatenate(powers[2] + [powers[1][0], powers[0][0], stays[1], stays[0]], axis=0)
    gathered = stack_parts(swap_blocks(gathered), 2, 192)
    for tile in range(M // TILE):
        at = pl.ds(tile * TILE, TILE)
        found = dot(gathered, point_ref[:, at], NN)
        found = found[0:96] + found[96:192]
        states = state_ref[:, at]
        last = jnp.zeros((S, TILE), F32)
        for s in range(S):
            last = jnp.where(states == s, found[s * S : (s + 1) * S], last)
        held = iota((S, TILE), 0) == states
        second = jnp.sum(jnp.where(held, found[80:88], 0.0), axis=0, keepdims=True)
        first = jnp.sum(jnp.where(held, found[88:96], 0.0), axis=0, keepdims=True)
        start = (states == 0).astype(F32)
        lapsed = dot(start_lapse, point_ref[:, at], NN)
        lapse1_ref[:, at] = (lapsed[:C] + lapsed[C:]) * start
        table_ref[0:8, at] = last
        table_ref[8:16, at] = found[0:8]
        table_ref[16:24, at] = found[64:72]
        table_ref[24:32, at] = found[72:80]
        table_ref[32:40, at] = jnp.concatenate(
            [start, first, second, account_ref[:, at], jnp.zeros((4, TILE), F32)], axis=0
        )
    stores = [
        pltpu.make_async_copy(src, dst, store_sem.at[n])
        for n, (src, dst) in enumerate(
            [
                (pre_ref, pre_hbm),
                (table_ref, table_hbm),
                (lapse1_ref, lapse1_hbm),
                (point_ref, point_hbm),
                (small_ref, small_hbm),
            ]
        )
    ]
    for store in stores[:4]:
        store.start()

    wait_from(
        b_peers, lambda peer: b_src.at[pair(peer)], lambda peer: b_buf.at[peer[0]], b_sems, lambda peer: peer[0]
    )
    total = b_buf[0]
    for slot in range(1, MP):
        total = total + b_buf[slot]
    rows = pl.ds(pl.multiple_of(months * KD, KD), KD)
    c_buf[rows, :] = total
    sends += send_to(c_peers, lambda peer: c_buf.at[rows, :], c_buf.at[rows, :], c_sems, sc)

    wait_from(
        b_peers, lambda peer: e_src.at[pair(peer)], lambda peer: e_buf.at[peer[0]], e_sems, lambda peer: peer[0]
    )
    early = e_buf[0]
    for slot in range(1, MP):
        early = early + e_buf[slot]
    early = jnp.transpose(jnp.concatenate([early, jnp.zeros((C - 8, C), F32)], axis=0))
    income = early[GQ : 2 * GQ]
    mine = pl.ds(pl.multiple_of(own * GQ, GQ), GQ)
    columns = cols_ref[mine, :]
    guarantee, spread, lapse_base = columns[:, 0:1], columns[:, 1:2], columns[:, 2:3]
    stay = [columns[:, 3:4], columns[:, 4:5]]
    pay = [columns[:, 5:6], columns[:, 6:7], columns[:, 7:8]]
    credited = first_ref[mine, :]

    def rows_at(peer):
        return pl.ds(pl.multiple_of(months_of(peer[1], zh) * KD, KD), KD)

    wait_from(
        c_peers, lambda peer: c_buf.at[rows, :], lambda peer: c_buf.at[rows_at(peer), :], c_sems, lambda peer: peer[1]
    )
    worth = jnp.transpose(c_buf[...])
    assets = []
    for date in range(DATES):
        pieces = stack_parts(worth[date * GQ : (date + 1) * GQ], 3, 3 * GQ)
        high = dot(pieces, disc_ref[date, 0], NN)
        middle = dot(pieces[: 2 * GQ], disc_ref[date, 1], NN)
        low = dot(pieces[:GQ], disc_ref[date, 2], NN)
        assets.append(
            high[:GQ] + ((high[GQ : 2 * GQ] + middle[:GQ]) + (high[2 * GQ :] + middle[GQ:] + low))
        )

    growth = jnp.ones((GQ, C), F32)
    present = jnp.zeros((GQ, C), F32)
    lapses = []
    for month in range(MONTHS):
        factor = lapse_base * 2.0 * jax.nn.sigmoid(LAPSE_SLOPE * (rates[month : month + 1] - credited))
        mass = early[:GQ, month : month + 1]
        for lag, lapse in enumerate(reversed(lapses)):
            mass = mass - lapse * stay[lag]
        lapses.append(mass * factor)
        growth = growth * (1.0 + credited / 12.0)
        paid = early[:GQ, 3 + month : 4 + month]
        for lag, lapse in enumerate(reversed(lapses)):
            paid = paid - lapse * pay[lag]
        flows = growth * (lapses[-1] + paid)
        held = assets[month]
        later = assets[month + 1] + income[:, month : month + 1]
        earned = 12.0 * (later - held) / held
        credited = jnp.maximum(
            guarantee, 0.5 * credited + 0.5 * (earned - spread) - LIQUID_CHARGE * flows / held
        )
        if month < MONTHS - 1:
            d_src[:, month * C : (month + 1) * C] = credited
        present = present + flows * jnp.exp(-rates[month + 1 : month + 2] * ((month + 1) / 12.0))
    sends += send_to(d_peers, lambda peer: d_src, rho_hbm.at[mine, :], d_sems, own)
    stores.append(pltpu.make_async_copy(d_src, rho_hbm.at[mine, :], store_sem.at[5]))
    stores[5].start()
    sums = dot(jnp.ones((8, C), F32), jnp.concatenate([present, jnp.zeros((C - GQ, C), F32)], axis=0), NT, EXACT)
    f_src[0] = sums
    f_src[1] = pltpu.roll(sums, C - 16, 1)
    sends += send_to(a_peers, lambda peer: f_src.at[peer[0] // 2 % 2], value_hbm.at[sc], f_sems, sc)
    stores.append(pltpu.make_async_copy(f_src.at[zh], value_hbm.at[sc], store_sem.at[6]))
    stores[6].start()
    small_ref[0:16, :] = 100.0 * jnp.where(zh == 0, credited[:16], credited[16:])
    stores[4].start()

    def pair_rows(peer):
        return pl.ds(pl.multiple_of(pair(peer) * GQ, GQ), GQ)

    wait_from(d_peers, lambda peer: d_src, lambda peer: rho_hbm.at[pair_rows(peer), :], d_sems, pair)
    wait_from(
        a_peers, lambda peer: f_src.at[peer[0] // 2 % 2], lambda peer: value_hbm.at[peer[1]], f_sems, lambda peer: peer[1]
    )
    for store in stores:
        store.wait()
    for copy in sends:
        copy.wait_send()


CHUNK = 32


def output_kernel(
    rho_hbm, pre_hbm, table_hbm, lapse1_hbm, point_hbm, small_hbm, value_hbm,
    occupancy_hbm, account_hbm, credited_ref, value_ref,
    rho_ref, pre_ref, table_ref, lapse1_ref, point_ref, small_ref, sums_ref,
    occupancy_ref, account_ref, load_sem, store_sem,
):
    loads = [
        pltpu.make_async_copy(src, dst, load_sem.at[n])
        for n, (src, dst) in enumerate(
            [
                (rho_hbm, rho_ref),
                (pre_hbm, pre_ref),
                (small_hbm, small_ref),
                (point_hbm, point_ref),
                (table_hbm, table_ref),
                (lapse1_hbm, lapse1_ref),
                (value_hbm, sums_ref),
            ]
        )
    ]
    for load in loads:
        load.start()
    for load in loads[:3]:
        load.wait()
    credited_ref[...] = small_ref[0:16, :]
    twice = pre_ref[0]
    rho = [pre_ref[1], rho_ref[:, :C], rho_ref[:, C:]]
    tables = []
    for month in (1, 2):
        rates = small_ref[24 + month : 25 + month, :]
        tables.append(twice * jax.nn.sigmoid(LAPSE_SLOPE * (rates - rho[month])))
    grown = [rate * (1.0 / 12.0) for rate in rho]
    gain = grown[0] + grown[1] + grown[0] * grown[1]
    tables.append(gain + grown[2] + gain * grown[2])
    tables = [parts(jnp.transpose(table), 2) for table in tables]

    for load in loads[3:]:
        load.wait()
    value = sums_ref[0]
    for slot in range(1, SC):
        value = value + sums_ref[slot]
    value_ref[...] = value[0:1, 0:16] * (1.0 / SCEN)
    copies = []
    for chunk in range(C // CHUNK):
        rows = slice(chunk * CHUNK, (chunk + 1) * CHUNK)
        lhs = jnp.concatenate([piece[rows] for table in tables for piece in table], axis=0)
        for tile in range(M // TILE):
            at = pl.ds(tile * TILE, TILE)
            found = dot(lhs, point_ref[:, at], NN)
            found = [
                found[2 * n * CHUNK : (2 * n + 1) * CHUNK] + found[(2 * n + 1) * CHUNK : (2 * n + 2) * CHUNK]
                for n in range(3)
            ]
            first = lapse1_ref[rows, at]
            second = (table_ref[33:34, at] - first * table_ref[24:25, at]) * found[0]
            third = (table_ref[34:35, at] - first * table_ref[16:17, at] - second * table_ref[24:25, at]) * found[1]
            for u in range(S):
                occupancy_ref[u, rows, at] = (
                    table_ref[u : u + 1, at]
                    - first * table_ref[8 + u : 9 + u, at]
                    - second * table_ref[16 + u : 17 + u, at]
                    - third * table_ref[24 + u : 25 + u, at]
                )
            account = table_ref[35:36, at]
            account_ref[rows, at] = account + account * found[2]
        copies.append(
            pltpu.make_async_copy(occupancy_ref.at[:, rows, :], occupancy_hbm.at[:, rows, :], store_sem.at[0, chunk])
        )
        copies.append(pltpu.make_async_copy(account_ref.at[rows, :], account_hbm.at[rows, :], store_sem.at[1, chunk]))
        copies[-2].start()
        copies[-1].start()
    for copy in copies:
        copy.wait()


def vmem(*shape):
    return pltpu.VMEM(shape, F32)


def body(
    group_id,
    issue_state,
    account_start,
    transition,
    lapse_base,
    benefit,
    bond_block,
    bond_flows,
    bond_target,
    base_rate,
    rate_moves,
    guarantee,
    spread,
    start_rate,
):
    in_vmem = pl.BlockSpec(memory_space=pltpu.VMEM)
    in_hbm = pl.BlockSpec(memory_space=pltpu.HBM)
    dma = pltpu.SemaphoreType.DMA
    between = pl.pallas_call(
        exchange_kernel,
        out_shape=[
            jax.ShapeDtypeStruct((PG, 2 * C), F32),
            jax.ShapeDtypeStruct((2, PG, C), F32),
            jax.ShapeDtypeStruct((40, M), F32),
            jax.ShapeDtypeStruct((C, M), F32),
            jax.ShapeDtypeStruct((PG, M), BF16),
            jax.ShapeDtypeStruct((32, C), F32),
            jax.ShapeDtypeStruct((SC, 8, C), F32),
        ],
        in_specs=[in_hbm] * 14,
        out_specs=[in_hbm] * 7,
        scratch_shapes=[
            vmem(2, PG, C),
            vmem(40, M),
            vmem(C, M),
            pltpu.VMEM((PG, M), BF16),
            vmem(32, C),
            vmem(1, C),
            vmem(MONTHS, C),
            pltpu.VMEM((1, B), jnp.int32),
            vmem(B, K),
            pltpu.VMEM((1, M), jnp.int32),
            pltpu.VMEM((1, M), jnp.int32),
            vmem(1, M),
            vmem(S, S, PG),
            vmem(1, S),
            vmem(1, PG),
            vmem(1, PG),
            vmem(1, PG),
            vmem(B // C, C),
            vmem(C, PG),
            pltpu.VMEM((3, B, K), BF16),
            vmem(KD, B),
            pltpu.VMEM((PG, B), BF16),
            pltpu.VMEM((DATES, 3, K, C), BF16),
            vmem(PG, 8),
            vmem(PG, C),
            vmem(8, C),
            vmem(SC, 8, C),
            vmem(MP // 2, 8, C),
            vmem(MP, 8, C),
            vmem(MP // 2, KD, C),
            vmem(MP, KD, C),
            vmem(K, C),
            vmem(GQ, 2 * C),
            vmem(2, 8, C),
            dma((14,)), dma((7,)),
            dma((SC,)), dma((SC,)),
            dma((MP,)), dma((MP,)),
            dma((MP,)), dma((MP,)),
            dma((SC,)), dma((SC,)),
            dma((MP,)), dma((MP,)),
            dma((SC,)), dma((SC,)),
        ],
        compiler_params=pltpu.CompilerParams(
            collective_id=0, has_side_effects=True, vmem_limit_bytes=VMEM_LIMIT
        ),
        name="exchange",
    )(
        base_rate.reshape(1, C),
        rate_moves,
        bond_block.reshape(1, B),
        bond_flows,
        group_id.reshape(1, M),
        issue_state.reshape(1, M),
        account_start.reshape(1, M),
        transition.transpose(1, 2, 0),
        benefit.reshape(1, S),
        guarantee.reshape(1, PG),
        spread.reshape(1, PG),
        lapse_base.reshape(1, PG),
        bond_target.reshape(B // C, C),
        start_rate,
    )
    occupancy, account_value, credited, value = pl.pallas_call(
        output_kernel,
        out_shape=[
            jax.ShapeDtypeStruct((S, C, M), F32),
            jax.ShapeDtypeStruct((C, M), F32),
            jax.ShapeDtypeStruct((16, C), F32),
            jax.ShapeDtypeStruct((1, 16), F32),
        ],
        in_specs=[in_hbm] * 7,
        out_specs=[in_hbm, in_hbm, in_vmem, in_vmem],
        scratch_shapes=[
            vmem(PG, 2 * C),
            vmem(2, PG, C),
            vmem(40, M),
            vmem(C, M),
            pltpu.VMEM((PG, M), BF16),
            vmem(32, C),
            vmem(SC, 8, C),
            vmem(S, C, M),
            vmem(C, M),
            dma((7,)),
            dma((2, C // CHUNK)),
        ],
        compiler_params=pltpu.CompilerParams(vmem_limit_bytes=VMEM_LIMIT),
        name="outputs",
    )(*between)
    return occupancy, account_value, credited.T, value.reshape(16)


def solution(mesh):
    placed = (
        P("mp"),
        P("mp"),
        P("mp"),
        P(),
        P(),
        P(),
        P("mp", None),
        P("mp", None),
        P("mp"),
        P("scen"),
        P(None, "scen"),
        P(),
        P(),
        P("scen", None),
    )
    return jax.shard_map(
        body,
        mesh=mesh,
        in_specs=placed,
        out_specs=(P(None, "scen", "mp"), P("scen", "mp"), P("scen", "mp"), P("mp")),
        check_vma=False,
    )
```

time: 53.8 us -> 41.7 us (0.78)
  local copies, waits for them, and re-layouts: 8.94 us -> 0 us
  Pallas kernels: 43 us -> 40.9 us
  other arithmetic: 0.72 us -> 0 us
    unnamed x20 -> x0, local copies, waits for them, and re-layouts: 8.23 us -> none
    pallas_call x1, Pallas kernels: 39.4 us -> 36.1 us  [body(): pl.pallas_call(exchange_kernel, out_shape=[jax.ShapeDtypeStruct((PG, 2 *...]
    pallas_call x1, Pallas kernels: 3.6 us -> 4.81 us  [body(): pl.pallas_call(output_kernel, out_shape=[jax.ShapeDtypeStruct((S, C, M),...]
    another operation x1 -> x0, other arithmetic: 0.72 us -> none  [body(): jnp.stack([guarantee, spread, lapse_base])]
    reshape x1 -> x0, local copies, waits for them, and re-layouts: 0.71 us -> none  [body(): bond_target.reshape(1, B)]
where the time goes in v3:
time: 41.7 us; the launch traced here: 41.6 us
  Pallas kernels  40.9 us (98%)
  between operations  0.64 us (2%)
    pallas_call x1, Pallas kernels, body(): pl.pallas_call(exchange_kernel, out_shape=[jax.ShapeDtypeStruct((PG, 2 *...  36.1 us
    pallas_call x1, Pallas kernels, body(): pl.pallas_call(output_kernel, out_shape=[jax.ShapeDtypeStruct((S, C, M),...  4.81 us

profile of v3, /device:TPU:1, one launch (start us, length us, event | category | flops | bytes accessed | tf_op | source)
XLA Modules:
  0.0 41.6 jit_solution(11390024299048528793)
XLA Ops:
  0.6 36.1 %exchange.1 = (f32[256,256]{1,0:T(8,128)}, f32[2,256,128]{2,1,0:T(8,128)}, f32[40,1024]{1,0:T(8,128)}, f32[128,1024]{1,0:T(8,128)}, bf16[256,1024]{1,0:T(8,128)(...) custom-call(f32[1,128]{1,0:T(1,128)} %bitcast.22, f32[3,128]{1,0:T(4,128)} %moves_hbm.1, s32[1,2560]{1,0:T(1,128)} %bitcast.15, ...), custom_call_target="tpu_custom_call" | custom-call | tf_op jit(solution)/shard_map/exchange/pallas_call | solution.py:588
  36.8 4.8 %outputs.1 = (f32[8,128,1024]{2,1,0:T(8,128)}, f32[128,1024]{1,0:T(8,128)}, f32[16,128]{1,0:T(8,128)}, f32[1,16]{1,0:T(1,128)}) custom-call(f32[256,256]{1,0:T(8,128)} %get-tuple-element.15.rho_hbm, f32[2,256,128]{2,1,0:T(8,128)} %get-tuple-element.16.pre_hbm, f32[40,1024]{1,0:T(8,128)} %get-tuple-element.17.table_hbm, ...), custom_call_target="tpu_custom_call" | custom-call | tf_op jit(solution)/shard_map/outputs/pallas_call | solution.py:664

commit v4 on v3

--- a/solution.py
+++ b/solution.py
@@ -136,20 +136,15 @@
     d_src,
     f_src,
     load_sem,
-    store_sem,
-    a_send,
-    a_recv,
-    e_send,
-    e_recv,
-    b_send,
-    b_recv,
-    c_send,
-    c_recv,
-    d_send,
-    d_recv,
-    f_send,
-    f_recv,
+    a_sems,
+    b_sems,
+    c_sems,
+    d_first_sems,
+    d_second_sems,
+    e_sems,
+    f_sems,
 ):
+    d_sems = [d_first_sems, d_second_sems]
     mp, sc = lax.axis_index("mp"), lax.axis_index("scen")
     x, zh, core = mp // 4, mp // 2 % 2, mp % 2
     own = x * 2 + core
@@ -179,7 +174,8 @@
     d_peers = [(mp_index(dx, 0, dc), sc) for dx in (2, 1, 3, 0) for dc in (0, 1) if (dx, dc) != (0, 0)]
 
     barrier = pltpu.get_barrier_semaphore()
-    for peer in a_peers + b_peers + c_peers:
+    greeted = a_peers + b_peers + [peer for peer, (dz, dy) in zip(c_peers, steps) if dz in (1, 3)]
+    for peer in greeted:
         pl.semaphore_signal(barrier, inc=1, device_id=peer, device_id_type=MESH)
     loads = [
         pltpu.make_async_copy(src, dst, load_sem.at[n])
@@ -205,30 +201,28 @@
     for load in loads:
         load.start()
 
-    def send_to(peers, src, dst, sems, mark):
-        copies = [
+    def send_to(peers, src, dst, sems):
+        for peer in peers:
             pltpu.make_async_remote_copy(
-                src_ref=src(peer), dst_ref=dst, send_sem=sems[0].at[n], recv_sem=sems[1].at[mark],
+                src_ref=src(peer), dst_ref=dst, send_sem=sems.at[0], recv_sem=sems.at[1],
                 device_id=peer, device_id_type=MESH,
-            )
-            for n, peer in enumerate(peers)
-        ]
-        for copy in copies:
-            copy.start()
-        return copies
-
-    def wait_from(peers, src, slot, sems, mark):
-        for n, peer in enumerate(peers):
-            pltpu.make_async_remote_copy(
-                src_ref=src(peer), dst_ref=slot(peer), send_sem=sems[0].at[n], recv_sem=sems[1].at[mark(peer)],
-                device_id=peer, device_id_type=MESH,
-            ).wait_recv()
+            ).start()
+
+    def all_of(peers, span, sems):
+        return pltpu.make_async_remote_copy(
+            src_ref=span, dst_ref=span, send_sem=sems.at[0], recv_sem=sems.at[1],
+            device_id=peers[0], device_id_type=MESH,
+        )
 
     def pair(peer):
         return peer[0] // 4 * 2 + peer[0] % 2
 
-    a_sems, b_sems, c_sems = (a_send, a_recv), (b_send, b_recv), (c_send, c_recv)
-    d_sems, e_sems, f_sems = (d_send, d_recv), (e_send, e_recv), (f_send, f_recv)
+    a_all = all_of(a_peers, a_buf.at[: SC - 1], a_sems)
+    b_all = all_of(b_peers, b_buf.at[: MP - 1], b_sems)
+    c_all = all_of(c_peers, c_buf.at[: K - KD], c_sems)
+    d_alls = [all_of(d_peers, rho_hbm.at[month, : PG - GQ], d_sems[month]) for month in range(MONTHS - 1)]
+    e_all = all_of(b_peers, e_buf.at[: MP - 1], e_sems)
+    f_all = all_of(a_peers, value_hbm.at[: SC - 1], f_sems)
     months = months_of(sc, zh)
 
     for load in loads[:2]:
@@ -252,8 +246,8 @@
     sums = jnp.concatenate(sums, axis=0)
     a_src[...] = jnp.concatenate([sums[:, : K // 2], sums[:, K // 2 :]], axis=0)
 
-    pl.semaphore_wait(barrier, len(a_peers + b_peers + c_peers))
-    sends = send_to(a_peers, lambda peer: a_src, a_buf.at[sc], a_sems, sc)
+    pl.semaphore_wait(barrier, len(greeted))
+    send_to(a_peers, lambda peer: a_src, a_buf.at[sc], a_sems)
     a_buf[sc] = a_src[...]
 
     for load in loads[2:4]:
@@ -313,10 +307,10 @@
         e_src[q] = jnp.concatenate(
             [early[:, q * GQ : (q + 1) * GQ], income[:, q * GQ : (q + 1) * GQ], jnp.zeros((8, C - 2 * GQ), F32)], axis=1
         )
-    sends += send_to(b_peers, lambda peer: e_src.at[pair(peer)], e_buf.at[mp], e_sems, mp)
+    send_to(b_peers, lambda peer: e_src.at[pair(peer)], e_buf.at[mp], e_sems)
     e_buf[mp] = e_src[own]
 
-    wait_from(a_peers, lambda peer: a_src, lambda peer: a_buf.at[peer[1]], a_sems, lambda peer: peer[1])
+    a_all.wait_recv()
     mean = a_buf[0]
     for slot in range(1, SC):
         mean = mean + a_buf[slot]
@@ -342,7 +336,7 @@
         b_src[q] = jnp.concatenate(
             [worth[date * KD : (date + 1) * KD, q * GQ : (q + 1) * GQ] for date in range(DATES)], axis=1
         )
-    sends += send_to(b_peers, lambda peer: b_src.at[pair(peer)], b_buf.at[mp], b_sems, mp)
+    send_to(b_peers, lambda peer: b_src.at[pair(peer)], b_buf.at[mp], b_sems)
     b_buf[mp] = b_src[own]
 
     local = [guarantee_ref[...], spread_ref[...], lapse_ref[...], stays[0][0:1], stays[1][0:1], pays[0][0:1], pays[1][0:1], pays[2][0:1]]
@@ -380,33 +374,28 @@
             [start, first, second, account_ref[:, at], jnp.zeros((4, TILE), F32)], axis=0
         )
     stores = [
-        pltpu.make_async_copy(src, dst, store_sem.at[n])
+        pltpu.make_async_copy(src, dst, load_sem.at[n])
         for n, (src, dst) in enumerate(
             [
                 (pre_ref, pre_hbm),
                 (table_ref, table_hbm),
                 (lapse1_ref, lapse1_hbm),
                 (point_ref, point_hbm),
-                (small_ref, small_hbm),
             ]
         )
     ]
-    for store in stores[:4]:
+    for store in stores:
         store.start()
 
-    wait_from(
-        b_peers, lambda peer: b_src.at[pair(peer)], lambda peer: b_buf.at[peer[0]], b_sems, lambda peer: peer[0]
-    )
+    b_all.wait_recv()
     total = b_buf[0]
     for slot in range(1, MP):
         total = total + b_buf[slot]
     rows = pl.ds(pl.multiple_of(months * KD, KD), KD)
     c_buf[rows, :] = total
-    sends += send_to(c_peers, lambda peer: c_buf.at[rows, :], c_buf.at[rows, :], c_sems, sc)
-
-    wait_from(
-        b_peers, lambda peer: e_src.at[pair(peer)], lambda peer: e_buf.at[peer[0]], e_sems, lambda peer: peer[0]
-    )
+    send_to(c_peers, lambda peer: c_buf.at[rows, :], c_buf.at[rows, :], c_sems)
+
+    e_all.wait_recv()
     early = e_buf[0]
     for slot in range(1, MP):
         early = early + e_buf[slot]
@@ -419,26 +408,20 @@
     pay = [columns[:, 5:6], columns[:, 6:7], columns[:, 7:8]]
     credited = first_ref[mine, :]
 
-    def rows_at(peer):
-        return pl.ds(pl.multiple_of(months_of(peer[1], zh) * KD, KD), KD)
-
-    wait_from(
-        c_peers, lambda peer: c_buf.at[rows, :], lambda peer: c_buf.at[rows_at(peer), :], c_sems, lambda peer: peer[1]
-    )
+    c_all.wait_recv()
     worth = jnp.transpose(c_buf[...])
-    assets = []
-    for date in range(DATES):
+
+    def assets_at(date):
         pieces = stack_parts(worth[date * GQ : (date + 1) * GQ], 3, 3 * GQ)
         high = dot(pieces, disc_ref[date, 0], NN)
         middle = dot(pieces[: 2 * GQ], disc_ref[date, 1], NN)
         low = dot(pieces[:GQ], disc_ref[date, 2], NN)
-        assets.append(
-            high[:GQ] + ((high[GQ : 2 * GQ] + middle[:GQ]) + (high[2 * GQ :] + middle[GQ:] + low))
-        )
+        return high[:GQ] + ((high[GQ : 2 * GQ] + middle[:GQ]) + (high[2 * GQ :] + middle[GQ:] + low))
 
     growth = jnp.ones((GQ, C), F32)
     present = jnp.zeros((GQ, C), F32)
     lapses = []
+    held = assets_at(0)
     for month in range(MONTHS):
         factor = lapse_base * 2.0 * jax.nn.sigmoid(LAPSE_SLOPE * (rates[month : month + 1] - credited))
         mass = early[:GQ, month : month + 1]
@@ -450,38 +433,42 @@
         for lag, lapse in enumerate(reversed(lapses)):
             paid = paid - lapse * pay[lag]
         flows = growth * (lapses[-1] + paid)
-        held = assets[month]
-        later = assets[month + 1] + income[:, month : month + 1]
+        after = assets_at(month + 1)
+        later = after + income[:, month : month + 1]
         earned = 12.0 * (later - held) / held
         credited = jnp.maximum(
             guarantee, 0.5 * credited + 0.5 * (earned - spread) - LIQUID_CHARGE * flows / held
         )
         if month < MONTHS - 1:
-            d_src[:, month * C : (month + 1) * C] = credited
+            d_src[month] = credited
+            send_to(d_peers, lambda peer: d_src.at[month], rho_hbm.at[month, mine, :], d_sems[month])
+        held = after
         present = present + flows * jnp.exp(-rates[month + 1 : month + 2] * ((month + 1) / 12.0))
-    sends += send_to(d_peers, lambda peer: d_src, rho_hbm.at[mine, :], d_sems, own)
-    stores.append(pltpu.make_async_copy(d_src, rho_hbm.at[mine, :], store_sem.at[5]))
-    stores[5].start()
     sums = dot(jnp.ones((8, C), F32), jnp.concatenate([present, jnp.zeros((C - GQ, C), F32)], axis=0), NT, EXACT)
     f_src[0] = sums
     f_src[1] = pltpu.roll(sums, C - 16, 1)
-    sends += send_to(a_peers, lambda peer: f_src.at[peer[0] // 2 % 2], value_hbm.at[sc], f_sems, sc)
-    stores.append(pltpu.make_async_copy(f_src.at[zh], value_hbm.at[sc], store_sem.at[6]))
-    stores[6].start()
+    send_to(a_peers, lambda peer: f_src.at[peer[0] // 2 % 2], value_hbm.at[sc], f_sems)
     small_ref[0:16, :] = 100.0 * jnp.where(zh == 0, credited[:16], credited[16:])
-    stores[4].start()
-
-    def pair_rows(peer):
-        return pl.ds(pl.multiple_of(pair(peer) * GQ, GQ), GQ)
-
-    wait_from(d_peers, lambda peer: d_src, lambda peer: rho_hbm.at[pair_rows(peer), :], d_sems, pair)
-    wait_from(
-        a_peers, lambda peer: f_src.at[peer[0] // 2 % 2], lambda peer: value_hbm.at[peer[1]], f_sems, lambda peer: peer[1]
-    )
-    for store in stores:
+    late = [
+        pltpu.make_async_copy(src, dst, load_sem.at[4 + n])
+        for n, (src, dst) in enumerate(
+            [
+                (small_ref, small_hbm),
+                (f_src.at[zh], value_hbm.at[sc]),
+                (d_src.at[0], rho_hbm.at[0, mine, :]),
+                (d_src.at[1], rho_hbm.at[1, mine, :]),
+            ]
+        )
+    ]
+    for store in late:
+        store.start()
+    for exchange in (a_all, e_all, b_all, c_all):
+        exchange.wait_send()
+    for store in stores + late:
         store.wait()
-    for copy in sends:
-        copy.wait_send()
+    for exchange in (*d_alls, f_all):
+        exchange.wait_send()
+        exchange.wait_recv()
 
 
 CHUNK = 32
@@ -489,9 +476,9 @@
 
 def output_kernel(
     rho_hbm, pre_hbm, table_hbm, lapse1_hbm, point_hbm, small_hbm, value_hbm,
-    occupancy_hbm, account_hbm, credited_ref, value_ref,
+    occupancy_hbm, account_hbm, credited_hbm, out_value_hbm,
     rho_ref, pre_ref, table_ref, lapse1_ref, point_ref, small_ref, sums_ref,
-    occupancy_ref, account_ref, load_sem, store_sem,
+    occupancy_ref, account_ref, value_ref, load_sem, store_sem,
 ):
     loads = [
         pltpu.make_async_copy(src, dst, load_sem.at[n])
@@ -511,9 +498,10 @@
         load.start()
     for load in loads[:3]:
         load.wait()
-    credited_ref[...] = small_ref[0:16, :]
+    copies = [pltpu.make_async_copy(small_ref.at[0:16, :], credited_hbm, store_sem.at[0, C // CHUNK])]
+    copies[0].start()
     twice = pre_ref[0]
-    rho = [pre_ref[1], rho_ref[:, :C], rho_ref[:, C:]]
+    rho = [pre_ref[1], rho_ref[0], rho_ref[1]]
     tables = []
     for month in (1, 2):
         rates = small_ref[24 + month : 25 + month, :]
@@ -529,7 +517,8 @@
     for slot in range(1, SC):
         value = value + sums_ref[slot]
     value_ref[...] = value[0:1, 0:16] * (1.0 / SCEN)
-    copies = []
+    copies.append(pltpu.make_async_copy(value_ref, out_value_hbm, store_sem.at[1, C // CHUNK]))
+    copies[-1].start()
     for chunk in range(C // CHUNK):
         rows = slice(chunk * CHUNK, (chunk + 1) * CHUNK)
         lhs = jnp.concatenate([piece[rows] for table in tables for piece in table], axis=0)
@@ -582,13 +571,12 @@
     spread,
     start_rate,
 ):
-    in_vmem = pl.BlockSpec(memory_space=pltpu.VMEM)
     in_hbm = pl.BlockSpec(memory_space=pltpu.HBM)
     dma = pltpu.SemaphoreType.DMA
     between = pl.pallas_call(
         exchange_kernel,
         out_shape=[
-            jax.ShapeDtypeStruct((PG, 2 * C), F32),
+            jax.ShapeDtypeStruct((2, PG, C), F32),
             jax.ShapeDtypeStruct((2, PG, C), F32),
             jax.ShapeDtypeStruct((40, M), F32),
             jax.ShapeDtypeStruct((C, M), F32),
@@ -631,15 +619,10 @@
             vmem(MP // 2, KD, C),
             vmem(MP, KD, C),
             vmem(K, C),
-            vmem(GQ, 2 * C),
+            vmem(2, GQ, C),
             vmem(2, 8, C),
-            dma((14,)), dma((7,)),
-            dma((SC,)), dma((SC,)),
-            dma((MP,)), dma((MP,)),
-            dma((MP,)), dma((MP,)),
-            dma((SC,)), dma((SC,)),
-            dma((MP,)), dma((MP,)),
-            dma((SC,)), dma((SC,)),
+            dma((14,)),
+            *[dma((2,)) for _ in range(7)],
         ],
         compiler_params=pltpu.CompilerParams(
             collective_id=0, has_side_effects=True, vmem_limit_bytes=VMEM_LIMIT
@@ -670,9 +653,9 @@
             jax.ShapeDtypeStruct((1, 16), F32),
         ],
         in_specs=[in_hbm] * 7,
-        out_specs=[in_hbm, in_hbm, in_vmem, in_vmem],
+        out_specs=[in_hbm] * 4,
         scratch_shapes=[
-            vmem(PG, 2 * C),
+            vmem(2, PG, C),
             vmem(2, PG, C),
             vmem(40, M),
             vmem(C, M),
@@ -681,8 +664,9 @@
             vmem(SC, 8, C),
             vmem(S, C, M),
             vmem(C, M),
+            vmem(1, 16),
             dma((7,)),
-            dma((2, C // CHUNK)),
+            dma((2, C // CHUNK + 1)),
         ],
         compiler_params=pltpu.CompilerParams(vmem_limit_bytes=VMEM_LIMIT),
         name="outputs",

time: 41.7 us -> 39.4 us (0.945)
  Pallas kernels: 40.9 us -> 38.6 us
    pallas_call x1, Pallas kernels: 36.1 us -> 34.3 us  [body(): pl.pallas_call(exchange_kernel, out_shape=[jax.ShapeDtypeStruct((2, PG, C...]
    pallas_call x1, Pallas kernels: 4.81 us -> 4.37 us  [body(): pl.pallas_call(output_kernel, out_shape=[jax.ShapeDtypeStruct((S, C, M),...]
where the time goes in v4:
time: 39.4 us; the launch traced here: 39.3 us
  Pallas kernels  38.6 us (98%)
  between operations  0.64 us (2%)
    pallas_call x1, Pallas kernels, body(): pl.pallas_call(exchange_kernel, out_shape=[jax.ShapeDtypeStruct((2, PG, C...  34.3 us
    pallas_call x1, Pallas kernels, body(): pl.pallas_call(output_kernel, out_shape=[jax.ShapeDtypeStruct((S, C, M),...  4.37 us

profile of v4, /device:TPU:1, one launch (start us, length us, event | category | flops | bytes accessed | tf_op | source)
XLA Modules:
  0.0 39.3 jit_solution(8588372542938521317)
XLA Ops:
  0.6 34.3 %exchange.1 = (f32[2,256,128]{2,1,0:T(8,128)}, f32[2,256,128]{2,1,0:T(8,128)}, f32[40,1024]{1,0:T(8,128)}, f32[128,1024]{1,0:T(8,128)}, bf16[256,1024]{1,0:T(8,1...) custom-call(f32[1,128]{1,0:T(1,128)} %bitcast.22, f32[3,128]{1,0:T(4,128)} %moves_hbm.1, s32[1,2560]{1,0:T(1,128)} %bitcast.15, ...), custom_call_target="tpu_custom_call" | custom-call | tf_op jit(solution)/shard_map/exchange/pallas_call | solution.py:576
  34.9 4.4 %outputs.1 = (f32[8,128,1024]{2,1,0:T(8,128)}, f32[128,1024]{1,0:T(8,128)}, f32[16,128]{1,0:T(8,128)}, f32[1,16]{1,0:T(1,128)}) custom-call(f32[2,256,128]{2,1,0:T(8,128)} %get-tuple-element.15.rho_hbm, f32[2,256,128]{2,1,0:T(8,128)} %get-tuple-element.16.pre_hbm, f32[40,1024]{1,0:T(8,128)} %get-tuple-element.17.table_hbm, ...), custom_call_target="tpu_custom_call" | custom-call | tf_op jit(solution)/shard_map/outputs/pallas_call | solution.py:647

commit v5 on v4

--- a/solution.py
+++ b/solution.py
@@ -98,13 +98,11 @@
     pre_hbm,
     table_hbm,
     lapse1_hbm,
-    point_hbm,
     small_hbm,
     value_hbm,
     pre_ref,
     table_ref,
     lapse1_ref,
-    point_ref,
     small_ref,
     base_ref,
     moves_ref,
@@ -123,6 +121,7 @@
     flow_parts,
     chosen_ref,
     bond_ref,
+    point_ref,
     disc_ref,
     cols_ref,
     first_ref,
@@ -174,7 +173,7 @@
     d_peers = [(mp_index(dx, 0, dc), sc) for dx in (2, 1, 3, 0) for dc in (0, 1) if (dx, dc) != (0, 0)]
 
     barrier = pltpu.get_barrier_semaphore()
-    greeted = a_peers + b_peers + [peer for peer, (dz, dy) in zip(c_peers, steps) if dz in (1, 3)]
+    greeted = a_peers + b_peers
     for peer in greeted:
         pl.semaphore_signal(barrier, inc=1, device_id=peer, device_id_type=MESH)
     loads = [
@@ -260,15 +259,15 @@
     def prepare(tile, income):
         at = pl.ds(pl.multiple_of(tile * TILE, TILE), TILE)
         pieces = parts(flows_ref[at, :], 3)
-        for number, piece in enumerate(pieces):
-            flow_parts[number, at, :] = piece
+        for number in range(2):
+            flow_parts[number, at, :] = pieces[number]
         found = dot(chosen, pieces[2], NT) + dot(chosen, pieces[1], NT) + dot(chosen, pieces[0], NT)
         chosen_ref[:, at] = found[:KD]
         groups = (bond_labels == block_ref[:, at]).astype(BF16)
         bond_ref[:, at] = groups
         return income + dot(stack_parts(found[KD : KD + 8], 3, 32), groups, NT)
 
-    income = lax.fori_loop(0, B // TILE, prepare, jnp.zeros((32, PG), F32))
+    income = lax.fori_loop(0, B // TILE, prepare, jnp.zeros((32, PG), F32), unroll=2)
     income = income[0:8] + income[8:16] + income[16:24]
 
     for load in loads[4:]:
@@ -321,8 +320,7 @@
         at = pl.ds(pl.multiple_of(tile * TILE, TILE), TILE)
         high = dot(mean, flow_parts[0, at, :], NT)
         middle = dot(mean, flow_parts[1, at, :], NT)
-        low = dot(mean, flow_parts[2, at, :], NT)
-        price = high[0:4] + ((high[4:8] + middle[0:4]) + (high[8:12] + middle[4:8] + low[0:4]))
+        price = high[0:4] + ((high[4:8] + middle[0:4]) + (high[8:12] + middle[4:8]))
         target = [target_ref[pl.ds(tile * 2 + n, 1), :] for n in range(2)]
         weight = jnp.concatenate(target, axis=1) / price
         flows = chosen_ref[:, at]
@@ -371,7 +369,8 @@
         table_ref[16:24, at] = found[64:72]
         table_ref[24:32, at] = found[72:80]
         table_ref[32:40, at] = jnp.concatenate(
-            [start, first, second, account_ref[:, at], jnp.zeros((4, TILE), F32)], axis=0
+            [start, first, second, account_ref[:, at], group_ref[:, at].astype(F32), jnp.zeros((3, TILE), F32)],
+            axis=0,
         )
     stores = [
         pltpu.make_async_copy(src, dst, load_sem.at[n])
@@ -380,7 +379,6 @@
                 (pre_ref, pre_hbm),
                 (table_ref, table_hbm),
                 (lapse1_ref, lapse1_hbm),
-                (point_ref, point_hbm),
             ]
         )
     ]
@@ -471,11 +469,11 @@
         exchange.wait_recv()
 
 
-CHUNK = 32
+CHUNK = 16
 
 
 def output_kernel(
-    rho_hbm, pre_hbm, table_hbm, lapse1_hbm, point_hbm, small_hbm, value_hbm,
+    rho_hbm, pre_hbm, table_hbm, lapse1_hbm, small_hbm, value_hbm,
     occupancy_hbm, account_hbm, credited_hbm, out_value_hbm,
     rho_ref, pre_ref, table_ref, lapse1_ref, point_ref, small_ref, sums_ref,
     occupancy_ref, account_ref, value_ref, load_sem, store_sem,
@@ -487,9 +485,9 @@
                 (rho_hbm, rho_ref),
                 (pre_hbm, pre_ref),
                 (small_hbm, small_ref),
-                (point_hbm, point_ref),
                 (table_hbm, table_ref),
-                (lapse1_hbm, lapse1_ref),
+                (lapse1_hbm.at[:CHUNK], lapse1_ref.at[:CHUNK]),
+                (lapse1_hbm.at[CHUNK:], lapse1_ref.at[CHUNK:]),
                 (value_hbm, sums_ref),
             ]
         )
@@ -498,7 +496,7 @@
         load.start()
     for load in loads[:3]:
         load.wait()
-    copies = [pltpu.make_async_copy(small_ref.at[0:16, :], credited_hbm, store_sem.at[0, C // CHUNK])]
+    copies = [pltpu.make_async_copy(small_ref.at[0:16, :], credited_hbm, store_sem.at[2])]
     copies[0].start()
     twice = pre_ref[0]
     rho = [pre_ref[1], rho_ref[0], rho_ref[1]]
@@ -511,14 +509,12 @@
     tables.append(gain + grown[2] + gain * grown[2])
     tables = [parts(jnp.transpose(table), 2) for table in tables]
 
-    for load in loads[3:]:
-        load.wait()
-    value = sums_ref[0]
-    for slot in range(1, SC):
-        value = value + sums_ref[slot]
-    value_ref[...] = value[0:1, 0:16] * (1.0 / SCEN)
-    copies.append(pltpu.make_async_copy(value_ref, out_value_hbm, store_sem.at[1, C // CHUNK]))
-    copies[-1].start()
+    loads[3].wait()
+    labels = group_at(iota((PG, TILE), 0)).astype(F32)
+    for tile in range(M // TILE):
+        at = pl.ds(tile * TILE, TILE)
+        point_ref[:, at] = (labels == table_ref[36:37, at]).astype(BF16)
+    loads[4].wait()
     for chunk in range(C // CHUNK):
         rows = slice(chunk * CHUNK, (chunk + 1) * CHUNK)
         lhs = jnp.concatenate([piece[rows] for table in tables for piece in table], axis=0)
@@ -541,12 +537,19 @@
                 )
             account = table_ref[35:36, at]
             account_ref[rows, at] = account + account * found[2]
-        copies.append(
-            pltpu.make_async_copy(occupancy_ref.at[:, rows, :], occupancy_hbm.at[:, rows, :], store_sem.at[0, chunk])
-        )
-        copies.append(pltpu.make_async_copy(account_ref.at[rows, :], account_hbm.at[rows, :], store_sem.at[1, chunk]))
-        copies[-2].start()
-        copies[-1].start()
+        pltpu.make_async_copy(occupancy_ref.at[:, rows, :], occupancy_hbm.at[:, rows, :], store_sem.at[0]).start()
+        pltpu.make_async_copy(account_ref.at[rows, :], account_hbm.at[rows, :], store_sem.at[1]).start()
+        if chunk == 0:
+            for load in loads[5:]:
+                load.wait()
+            value = sums_ref[0]
+            for slot in range(1, SC):
+                value = value + sums_ref[slot]
+            value_ref[...] = value[0:1, 0:16] * (1.0 / SCEN)
+            copies.append(pltpu.make_async_copy(value_ref, out_value_hbm, store_sem.at[3]))
+            copies[-1].start()
+    copies.append(pltpu.make_async_copy(occupancy_ref, occupancy_hbm, store_sem.at[0]))
+    copies.append(pltpu.make_async_copy(account_ref, account_hbm, store_sem.at[1]))
     for copy in copies:
         copy.wait()
 
@@ -580,17 +583,15 @@
             jax.ShapeDtypeStruct((2, PG, C), F32),
             jax.ShapeDtypeStruct((40, M), F32),
             jax.ShapeDtypeStruct((C, M), F32),
-            jax.ShapeDtypeStruct((PG, M), BF16),
             jax.ShapeDtypeStruct((32, C), F32),
             jax.ShapeDtypeStruct((SC, 8, C), F32),
         ],
         in_specs=[in_hbm] * 14,
-        out_specs=[in_hbm] * 7,
+        out_specs=[in_hbm] * 6,
         scratch_shapes=[
             vmem(2, PG, C),
             vmem(40, M),
             vmem(C, M),
-            pltpu.VMEM((PG, M), BF16),
             vmem(32, C),
             vmem(1, C),
             vmem(MONTHS, C),
@@ -606,9 +607,10 @@
             vmem(1, PG),
             vmem(B // C, C),
             vmem(C, PG),
-            pltpu.VMEM((3, B, K), BF16),
+            pltpu.VMEM((2, B, K), BF16),
             vmem(KD, B),
             pltpu.VMEM((PG, B), BF16),
+            pltpu.VMEM((PG, M), BF16),
             pltpu.VMEM((DATES, 3, K, C), BF16),
             vmem(PG, 8),
             vmem(PG, C),
@@ -652,7 +654,7 @@
             jax.ShapeDtypeStruct((16, C), F32),
             jax.ShapeDtypeStruct((1, 16), F32),
         ],
-        in_specs=[in_hbm] * 7,
+        in_specs=[in_hbm] * 6,
         out_specs=[in_hbm] * 4,
         scratch_shapes=[
             vmem(2, PG, C),
@@ -666,7 +668,7 @@
             vmem(C, M),
             vmem(1, 16),
             dma((7,)),
-            dma((2, C // CHUNK + 1)),
+            dma((4,)),
         ],
         compiler_params=pltpu.CompilerParams(vmem_limit_bytes=VMEM_LIMIT),
         name="outputs",

time: 39.4 us -> 37.7 us (0.957)
  Pallas kernels: 38.6 us -> 37 us
    pallas_call x1, Pallas kernels: 34.3 us -> 32.8 us  [body(): pl.pallas_call(exchange_kernel, out_shape=[jax.ShapeDtypeStruct((2, PG, C...]
where the time goes in v5:
time: 37.7 us; the launch traced here: 37.6 us
  Pallas kernels  37 us (98%)
  between operations  0.64 us (2%)
    pallas_call x1, Pallas kernels, body(): pl.pallas_call(exchange_kernel, out_shape=[jax.ShapeDtypeStruct((2, PG, C...  32.8 us
    pallas_call x1, Pallas kernels, body(): pl.pallas_call(output_kernel, out_shape=[jax.ShapeDtypeStruct((S, C, M),...  4.2 us

profile of v5, /device:TPU:1, one launch (start us, length us, event | category | flops | bytes accessed | tf_op | source)
XLA Modules:
  0.0 37.6 jit_solution(10355094154619858942)
XLA Ops:
  0.6 32.8 %exchange.1 = (f32[2,256,128]{2,1,0:T(8,128)}, f32[2,256,128]{2,1,0:T(8,128)}, f32[40,1024]{1,0:T(8,128)}, f32[128,1024]{1,0:T(8,128)}, f32[32,128]{1,0:T(8,128)}, /*index=5*/f32[16,8,128]{2,1,0:T(8,128)}) custom-call(f32[1,128]{1,0:T(1,128)} %bitcast.22, f32[3,128]{1,0:T(4,128)} %moves_hbm.1, s32[1,2560]{1,0:T(1,128)} %bitcast.15, f32[2560,256]{1,0:T(8,128)} %flows_hbm.1, ...), custom_call_target="tpu_custom_call" | custom-call | tf_op jit(solution)/shard_map/exchange/pallas_call | solution.py:579
  33.4 4.2 %outputs.1 = (f32[8,128,1024]{2,1,0:T(8,128)}, f32[128,1024]{1,0:T(8,128)}, f32[16,128]{1,0:T(8,128)}, f32[1,16]{1,0:T(1,128)}) custom-call(f32[2,256,128]{2,1,0:T(8,128)} %get-tuple-element.14.rho_hbm, f32[2,256,128]{2,1,0:T(8,128)} %get-tuple-element.15.pre_hbm, f32[40,1024]{1,0:T(8,128)} %get-tuple-element.16.table_hbm, ...), custom_call_target="tpu_custom_call" | custom-call | tf_op jit(solution)/shard_map/outputs/pallas_call | solution.py:649

commit v6 on v5

--- a/solution.py
+++ b/solution.py
@@ -260,7 +260,7 @@
         at = pl.ds(pl.multiple_of(tile * TILE, TILE), TILE)
         pieces = parts(flows_ref[at, :], 3)
         for number in range(2):
-            flow_parts[number, at, :] = pieces[number]
+            flow_parts[number, :, at] = jnp.transpose(pieces[number])
         found = dot(chosen, pieces[2], NT) + dot(chosen, pieces[1], NT) + dot(chosen, pieces[0], NT)
         chosen_ref[:, at] = found[:KD]
         groups = (bond_labels == block_ref[:, at]).astype(BF16)
@@ -318,8 +318,8 @@
 
     def weigh(tile, total):
         at = pl.ds(pl.multiple_of(tile * TILE, TILE), TILE)
-        high = dot(mean, flow_parts[0, at, :], NT)
-        middle = dot(mean, flow_parts[1, at, :], NT)
+        high = dot(mean, flow_parts[0, :, at], NN)
+        middle = dot(mean, flow_parts[1, :, at], NN)
         price = high[0:4] + ((high[4:8] + middle[0:4]) + (high[8:12] + middle[4:8]))
         target = [target_ref[pl.ds(tile * 2 + n, 1), :] for n in range(2)]
         weight = jnp.concatenate(target, axis=1) / price
@@ -482,10 +482,10 @@
         pltpu.make_async_copy(src, dst, load_sem.at[n])
         for n, (src, dst) in enumerate(
             [
+                (table_hbm, table_ref),
                 (rho_hbm, rho_ref),
                 (pre_hbm, pre_ref),
                 (small_hbm, small_ref),
-                (table_hbm, table_ref),
                 (lapse1_hbm.at[:CHUNK], lapse1_ref.at[:CHUNK]),
                 (lapse1_hbm.at[CHUNK:], lapse1_ref.at[CHUNK:]),
                 (value_hbm, sums_ref),
@@ -494,7 +494,12 @@
     ]
     for load in loads:
         load.start()
-    for load in loads[:3]:
+    loads[0].wait()
+    labels = group_at(iota((PG, TILE), 0)).astype(F32)
+    for tile in range(M // TILE):
+        at = pl.ds(tile * TILE, TILE)
+        point_ref[:, at] = (labels == table_ref[36:37, at]).astype(BF16)
+    for load in loads[1:4]:
         load.wait()
     copies = [pltpu.make_async_copy(small_ref.at[0:16, :], credited_hbm, store_sem.at[2])]
     copies[0].start()
@@ -509,11 +514,6 @@
     tables.append(gain + grown[2] + gain * grown[2])
     tables = [parts(jnp.transpose(table), 2) for table in tables]
 
-    loads[3].wait()
-    labels = group_at(iota((PG, TILE), 0)).astype(F32)
-    for tile in range(M // TILE):
-        at = pl.ds(tile * TILE, TILE)
-        point_ref[:, at] = (labels == table_ref[36:37, at]).astype(BF16)
     loads[4].wait()
     for chunk in range(C // CHUNK):
         rows = slice(chunk * CHUNK, (chunk + 1) * CHUNK)
@@ -607,7 +607,7 @@
             vmem(1, PG),
             vmem(B // C, C),
             vmem(C, PG),
-            pltpu.VMEM((2, B, K), BF16),
+            pltpu.VMEM((2, K, B), BF16),
             vmem(KD, B),
             pltpu.VMEM((PG, B), BF16),
             pltpu.VMEM((PG, M), BF16),

time: 37.7 us -> 37.1 us (0.984)
  Pallas kernels: 37 us -> 36.3 us
    pallas_call x1, Pallas kernels: 32.8 us -> 32.2 us  [body(): pl.pallas_call(exchange_kernel, out_shape=[jax.ShapeDtypeStruct((2, PG, C...]
where the time goes in v6:
time: 37.1 us; the launch traced here: 37 us
  Pallas kernels  36.3 us (98%)
  between operations  0.64 us (2%)
    pallas_call x1, Pallas kernels, body(): pl.pallas_call(exchange_kernel, out_shape=[jax.ShapeDtypeStruct((2, PG, C...  32.2 us
    pallas_call x1, Pallas kernels, body(): pl.pallas_call(output_kernel, out_shape=[jax.ShapeDtypeStruct((S, C, M),...  4.1 us

profile of v6, /device:TPU:1, one launch (start us, length us, event | category | flops | bytes accessed | tf_op | source)
XLA Modules:
  0.0 37.0 jit_solution(1846812741847754181)
XLA Ops:
  0.6 32.2 %exchange.1 = (f32[2,256,128]{2,1,0:T(8,128)}, f32[2,256,128]{2,1,0:T(8,128)}, f32[40,1024]{1,0:T(8,128)}, f32[128,1024]{1,0:T(8,128)}, f32[32,128]{1,0:T(8,128)}, /*index=5*/f32[16,8,128]{2,1,0:T(8,128)}) custom-call(f32[1,128]{1,0:T(1,128)} %bitcast.22, f32[3,128]{1,0:T(4,128)} %moves_hbm.1, s32[1,2560]{1,0:T(1,128)} %bitcast.15, f32[2560,256]{1,0:T(8,128)} %flows_hbm.1, ...), custom_call_target="tpu_custom_call" | custom-call | tf_op jit(solution)/shard_map/exchange/pallas_call | solution.py:579
  32.9 4.1 %outputs.1 = (f32[8,128,1024]{2,1,0:T(8,128)}, f32[128,1024]{1,0:T(8,128)}, f32[16,128]{1,0:T(8,128)}, f32[1,16]{1,0:T(1,128)}) custom-call(f32[2,256,128]{2,1,0:T(8,128)} %get-tuple-element.14.rho_hbm, f32[2,256,128]{2,1,0:T(8,128)} %get-tuple-element.15.pre_hbm, f32[40,1024]{1,0:T(8,128)} %get-tuple-element.16.table_hbm, ...), custom_call_target="tpu_custom_call" | custom-call | tf_op jit(solution)/shard_map/outputs/pallas_call | solution.py:649

commit v7 on v6

--- a/solution.py
+++ b/solution.py
@@ -306,7 +306,6 @@
         e_src[q] = jnp.concatenate(
             [early[:, q * GQ : (q + 1) * GQ], income[:, q * GQ : (q + 1) * GQ], jnp.zeros((8, C - 2 * GQ), F32)], axis=1
         )
-    send_to(b_peers, lambda peer: e_src.at[pair(peer)], e_buf.at[mp], e_sems)
     e_buf[mp] = e_src[own]
 
     a_all.wait_recv()
@@ -335,6 +334,7 @@
             [worth[date * KD : (date + 1) * KD, q * GQ : (q + 1) * GQ] for date in range(DATES)], axis=1
         )
     send_to(b_peers, lambda peer: b_src.at[pair(peer)], b_buf.at[mp], b_sems)
+    send_to(b_peers, lambda peer: e_src.at[pair(peer)], e_buf.at[mp], e_sems)
     b_buf[mp] = b_src[own]
 
     local = [guarantee_ref[...], spread_ref[...], lapse_ref[...], stays[0][0:1], stays[1][0:1], pays[0][0:1], pays[1][0:1], pays[2][0:1]]

time: 37.1 us -> 37.7 us (1.016)
  Pallas kernels: 36.3 us -> 36.9 us
    pallas_call x1, Pallas kernels: 32.2 us -> 32.9 us  [body(): pl.pallas_call(exchange_kernel, out_shape=[jax.ShapeDtypeStruct((2, PG, C...]
where the time goes in v7:
time: 37.7 us; the launch traced here: 37.6 us
  Pallas kernels  36.9 us (98%)
  between operations  0.64 us (2%)
    pallas_call x1, Pallas kernels, body(): pl.pallas_call(exchange_kernel, out_shape=[jax.ShapeDtypeStruct((2, PG, C...  32.9 us
    pallas_call x1, Pallas kernels, body(): pl.pallas_call(output_kernel, out_shape=[jax.ShapeDtypeStruct((S, C, M),...  4.1 us

profile of v7, /device:TPU:1, one launch (start us, length us, event | category | flops | bytes accessed | tf_op | source)
XLA Modules:
  0.0 37.6 jit_solution(7499111788316806202)
XLA Ops:
  0.6 32.9 %exchange.1 = (f32[2,256,128]{2,1,0:T(8,128)}, f32[2,256,128]{2,1,0:T(8,128)}, f32[40,1024]{1,0:T(8,128)}, f32[128,1024]{1,0:T(8,128)}, f32[32,128]{1,0:T(8,128)}, /*index=5*/f32[16,8,128]{2,1,0:T(8,128)}) custom-call(f32[1,128]{1,0:T(1,128)} %bitcast.22, f32[3,128]{1,0:T(4,128)} %moves_hbm.1, s32[1,2560]{1,0:T(1,128)} %bitcast.15, f32[2560,256]{1,0:T(8,128)} %flows_hbm.1, ...), custom_call_target="tpu_custom_call" | custom-call | tf_op jit(solution)/shard_map/exchange/pallas_call | solution.py:579
  33.5 4.1 %outputs.1 = (f32[8,128,1024]{2,1,0:T(8,128)}, f32[128,1024]{1,0:T(8,128)}, f32[16,128]{1,0:T(8,128)}, f32[1,16]{1,0:T(1,128)}) custom-call(f32[2,256,128]{2,1,0:T(8,128)} %get-tuple-element.14.rho_hbm, f32[2,256,128]{2,1,0:T(8,128)} %get-tuple-element.15.pre_hbm, f32[40,1024]{1,0:T(8,128)} %get-tuple-element.16.table_hbm, ...), custom_call_target="tpu_custom_call" | custom-call | tf_op jit(solution)/shard_map/outputs/pallas_call | solution.py:649
